TPU v7x, 128 devices: a whole 4x4x4 slice. The times are simulated.
128 devices in a mesh: surf: 128 (over z, y, x, core).
Axes of the slice: x: 4, y: 4, z: 4, core: 2. Of those that a mesh axis runs over, the one named last changes fastest.
Arguments:
- splat: float32 [11, 524288], P(None, 'surf'), may hold values from -4 to 4
- position: float32 [3, 524288], P(None, 'surf'), may hold values from -3 to 3
- harmonics: float32 [48, 524288], P(None, 'surf'), may hold values from -2 to 2
- cameras: float32 [4, 3], replicated, may hold values from 5 to 8
- tile_lists: int32 [4096, 256], P('surf'), may hold values from 0 to 524287, as said below
- tile_counts: int32 [4096], P('surf'), may hold values from 1 to 256, as said below
- target_color: float32 [3, 4096, 256], P(None, 'surf'), may hold values from 0 to 1
- target_normal: float32 [3, 4096, 256], P(None, 'surf'), may hold values from -3 to 3
Outputs:
- grad_splat: float32 [11, 524288], P(None, 'surf')
- grad_position: float32 [3, 524288], P(None, 'surf')
- grad_harmonics: float32 [48, 524288], P(None, 'surf')
- tile_loss: float32 [4096], P('surf')
Inputs may be any that keep to these rules, and one draw needn't show every extreme that they name: `tile_lists`: entries name surfels; among the live slots of the tiles of one device, exactly 32 * 192 / 128 name surfels of each block of 4096 consecutive surfel numbers, and among its padding slots exactly 32 * 64 / 128. `tile_counts`: the counts of one device's tiles sum to 6144; one tile of every device is full.
All inputs are finite; a program needn't handle non-finite values.
Results may differ from a plain program's by a relative error of at most 0.0003.
Values sent between devices are 32-bit elements; how exact they have to be, the bound alone decides.
A program may use at most 128 MiB of HBM per device.

v0:
```python
import math

import jax
import jax.numpy as jnp
from jax import lax
from jax.sharding import PartitionSpec as P

sh_zero = 0.28209479177387814
sh_one = 0.4886025119029199
sh_two = (
    1.0925484305920792,
    -1.0925484305920792,
    0.31539156525252005,
    -1.0925484305920792,
    0.5462742152960396,
)
sh_three = (
    -0.5900435899266435,
    2.890611442640554,
    -0.4570457994644658,
    0.3731763325901154,
    -0.4570457994644658,
    1.445305721320277,
    -0.5900435899266435,
)


def sh_color(centre, coeffs, camera):
    offset = centre - camera
    length = jnp.sqrt(jnp.sum(offset * offset, axis=0))
    xdir = offset[0] / length
    ydir = offset[1] / length
    zdir = offset[2] / length
    xsq = xdir * xdir
    ysq = ydir * ydir
    zsq = zdir * zdir
    basis = jnp.stack(
        [
            jnp.full_like(xdir, sh_zero),
            -sh_one * ydir,
            sh_one * zdir,
            -sh_one * xdir,
            sh_two[0] * xdir * ydir,
            sh_two[1] * ydir * zdir,
            sh_two[2] * (2.0 * zsq - xsq - ysq),
            sh_two[3] * xdir * zdir,
            sh_two[4] * (xsq - ysq),
            sh_three[0] * ydir * (3.0 * xsq - ysq),
            sh_three[1] * xdir * ydir * zdir,
            sh_three[2] * ydir * (4.0 * zsq - xsq - ysq),
            sh_three[3] * zdir * (2.0 * zsq - 3.0 * xsq - 3.0 * ysq),
            sh_three[4] * xdir * (4.0 * zsq - xsq - ysq),
            sh_three[5] * zdir * (xsq - ysq),
            sh_three[6] * xdir * (xsq - 3.0 * ysq),
        ],
        axis=0,
    )
    shaped = coeffs.reshape(3, 16, coeffs.shape[-1])
    return jnp.maximum(jnp.sum(shaped * basis[None], axis=1) + 0.5, 0.0)


def pick_camera(cameras, view):
    chosen = jnp.zeros((3, view.shape[0]), cameras.dtype)
    for which in range(4):
        chosen = jnp.where(view[None, :] == which, cameras[which][:, None], chosen)
    return chosen


def tile_loss_of(geom, colors, count, target, normals):
    pixel = jnp.arange(256, dtype=jnp.int32)
    px = ((pixel % 16).astype(geom.dtype) - 7.5) / 8.0
    py = ((pixel // 16).astype(geom.dtype) - 7.5) / 8.0
    ucoord = geom[0][None, :] + geom[1][None, :] * px[:, None] + geom[2][None, :] * py[:, None]
    vcoord = geom[3][None, :] + geom[4][None, :] * px[:, None] + geom[5][None, :] * py[:, None]
    live = (jnp.arange(256, dtype=jnp.int32) < count).astype(geom.dtype)
    alpha = (live * 0.95 * jax.nn.sigmoid(geom[6]))[None, :] * jnp.exp(
        -0.5 * (ucoord * ucoord + vcoord * vcoord)
    )
    logkeep = jnp.log(1.0 - alpha)
    trans = jnp.exp(jnp.cumsum(logkeep, axis=1) - logkeep)
    weight = alpha * trans
    render = jnp.einsum("pk,ck->cp", weight, colors, precision=lax.Precision.HIGHEST)
    color_term = jnp.sum((render - target) ** 2) / 256.0
    depth = geom[7][None, :]
    wdepth = weight * depth
    before_w = jnp.cumsum(weight, axis=1) - weight
    before_wd = jnp.cumsum(wdepth, axis=1) - wdepth
    distortion = jnp.sum(2.0 * weight * (depth * before_w - before_wd)) / 256.0
    facing = jnp.einsum("cp,ck->pk", normals, geom[8:11], precision=lax.Precision.HIGHEST)
    normal_term = jnp.sum(weight * (1.0 - facing)) / 256.0
    return color_term + distortion + 0.5 * normal_term


def all_tiles(geom, colors, tile_counts, target_color, target_normal):
    tile_grad = jax.vmap(jax.value_and_grad(tile_loss_of, argnums=(0, 1)))
    tiles_here = tile_counts.shape[0]
    group = math.gcd(tiles_here, 8)
    rounds = tiles_here // group

    def grouped(array, width):
        return jnp.transpose(array.reshape(width, rounds, group, 256), (1, 2, 0, 3))

    def one_group(items):
        value, grads = tile_grad(items[0], items[1], items[2], items[3], items[4])
        return (value, grads[0], grads[1])

    losses, dgeom, dcol = lax.map(
        one_group,
        (
            grouped(geom, 11),
            grouped(colors, 3),
            tile_counts.reshape(rounds, group),
            grouped(target_color, 3),
            grouped(target_normal, 3),
        ),
    )
    dgeom = jnp.transpose(dgeom, (2, 0, 1, 3)).reshape(11, tiles_here * 256)
    dcol = jnp.transpose(dcol, (2, 0, 1, 3)).reshape(3, tiles_here * 256)
    return (losses.reshape(tiles_here), dgeom, dcol)


def place_rows(values, order, slots):
    return jnp.zeros((values.shape[0], slots), values.dtype).at[:, order].set(values)


def on_device(
    splat, position, harmonics, cameras, tile_lists, tile_counts, target_color, target_normal
):
    devices = lax.axis_size("surf")
    tiles_here = tile_lists.shape[0]
    slots = tiles_here * 256
    surf_here = splat.shape[1]
    flat = tile_lists.reshape(-1)
    holder = flat // surf_here
    order = jnp.argsort(holder, stable=True)
    wanted = (flat % surf_here)[order]
    tile_global = lax.axis_index("surf") * tiles_here + jnp.arange(tiles_here, dtype=jnp.int32)
    tile_view = tile_global // (tiles_here * devices // 4)
    slot_view = jnp.repeat(tile_view, 256)
    got = lax.all_to_all(wanted, "surf", split_axis=0, concat_axis=0, tiled=True)
    payload = jnp.concatenate([splat[:, got], position[:, got], harmonics[:, got]], axis=0)
    arrived = place_rows(
        lax.all_to_all(payload, "surf", split_axis=1, concat_axis=1, tiled=True), order, slots
    )
    colored, color_back = jax.vjp(
        sh_color, arrived[11:14], arrived[14:], pick_camera(cameras, slot_view)
    )
    losses, dgeom, dcol = all_tiles(arrived[:11], colored, tile_counts, target_color, target_normal)
    slot_pos, slot_sh, unused = color_back(dcol)
    sent_back = jnp.concatenate([dgeom, slot_pos, slot_sh], axis=0)[:, order]
    returned = lax.all_to_all(sent_back, "surf", split_axis=1, concat_axis=1, tiled=True)
    dsplat = returned[:11]
    dpos = returned[11:14]
    dsh = returned[14:]
    grad_splat = jnp.zeros((11, surf_here), jnp.float32).at[:, got].add(dsplat)
    grad_position = jnp.zeros((3, surf_here), jnp.float32).at[:, got].add(dpos)
    grad_harmonics = jnp.zeros((48, surf_here), jnp.float32).at[:, got].add(dsh)
    return (grad_splat, grad_position, grad_harmonics, losses)


def solution(mesh):
    return jax.shard_map(
        on_device,
        mesh=mesh,
        in_specs=(
            P(None, "surf"),
            P(None, "surf"),
            P(None, "surf"),
            P(),
            P("surf", None),
            P("surf"),
            P(None, "surf", None),
            P(None, "surf", None),
        ),
        out_specs=(P(None, "surf"), P(None, "surf"), P(None, "surf"), P("surf")),
        check_vma=False,
    )
```

profile of v0, /device:TPU:1, one launch (start us, length us, event | category | flops | bytes accessed | tf_op | source)
XLA Modules:
  0.0 1240.7 jit_solution(18070557055956671435)
XLA Ops:
  8.3 45.5 %gather_fusion = s32[8192]{0:T(1024)S(1)} fusion(s32[8192]{0:T(1024)S(1)} %get-tuple-element.307, s32[8192]{0:T(1024)S(1)} %get-tuple-element.305), kind=kCustom, calls=%fused_computation | custom fusion | bytes 98304 | tf_op jit(solution)/shard_map/gather | solution.py:136
  54.5 11.5 all-to-all-start
  77.1 29.3 %gather_fusion.1 = f32[8192,11]{1,0:T(8,128)} fusion(f32[11,4096]{0,1:T(8,128)} %copy.276, s32[8192]{0:T(1024)S(1)} %broadcast_clamp_fusion), kind=kCustom, calls=%fused_computation.1 | custom fusion | bytes 753664 | tf_op jit(solution)/shard_map/gather | solution.py:141
  106.4 29.3 %gather_fusion.2 = f32[8192,3]{1,0:T(8,128)} fusion(f32[3,4096]{0,1:T(8,128)} %copy.277, s32[8192]{0:T(1024)S(1)} %broadcast_clamp_fusion), kind=kCustom, calls=%fused_computation.2 | custom fusion | bytes 229376 | tf_op jit(solution)/shard_map/gather | solution.py:141
  135.7 27.7 %gather_fusion.3 = f32[8192,48]{1,0:T(8,128)} fusion(f32[48,4096]{0,1:T(8,128)S(1)} %copy.278, s32[8192]{0:T(1024)S(1)} %broadcast_clamp_fusion), kind=kCustom, calls=%fused_computation.3 | custom fusion | bytes 3178496 | tf_op jit(solution)/shard_map/gather | solution.py:141
  163.4 8.9 pad_maximum_fusion
  186.2 29.0 %all-to-all-done.1 = f32[128,1,3968]{2,1,0:T(1,128)S(1)} async-done(((f32[128,1,3968]{2,1,0:T(1,128)}), f32[128,1,3968]{2,1,0:T(1,128)S(1)}, u32[]{:S(2)}, u32[]{:S(2)}) %all-to-all-start.1) | async-done | bytes 2031648 | tf_op jit(solution)/shard_map/all_to_all | solution.py:143
  231.6 23.3 %scatter_custom_fusion = f32[62,8192]{0,1:T(8,128)} fusion(s32[8192]{0:T(1024)S(1)} %get-tuple-element.304, f32[8192,62]{1,0:T(8,128)} %bitcast.314, f32[]{:T(128)} %constant.237.clone.1), kind=kCustom, calls=%fused_computation.158 | custom fusion | bytes 2032128 | tf_op jit(solution)/shard_map/scatter | solution.py:123
  275.9 707.4 %while.17 = (s32[]{:T(128)}, f32[4,8]{1,0:T(4,128)S(1)}, f32[4,8,11,256]{3,2,1,0:T(8,128)}, f32[4,8,3,256]{3,2,1,0:T(4,128)}, f32[4,8,3,256]{3,2,1,0:T(4,128)S(1...) while((s32[]{:T(128)}, f32[4,8]{1,0:T(4,128)S(1)}, ...), condition=%wide.region_29.30_spmd, body=%wide.region_4.29_spmd.sunk | while | flops 581700096 | bytes 176545584 | solution.py:107
  289.6 97.1 %fusion.184 = f32[8,256,2,128]{1,0,3,2:T(8,128)S(1)} fusion(f32[8,256,2,128]{1,0,3,2:T(8,128)S(1)} %get-tuple-element.435), kind=kOutput, calls=%fused_computation.279.clone.1 | output fusion | flops 66584576 | bytes 4194304 | tf_op jit(solution)/shard_map/reduce-window.50
  387.5 23.2 %fusion.180 = f32[8,256,2,128]{1,0,3,2:T(8,128)S(1)} fusion(f32[8,256,2,128]{1,0,3,2:T(8,128)S(1)} %get-tuple-element.435), kind=kOutput, calls=%fused_computation.41.clone.1 | output fusion | flops 67633152 | bytes 4194304 | tf_op jit(solution)/shard_map/reduce-window.54
  466.3 97.1 %fusion.184 = f32[8,256,2,128]{1,0,3,2:T(8,128)S(1)} fusion(f32[8,256,2,128]{1,0,3,2:T(8,128)S(1)} %get-tuple-element.435), kind=kOutput, calls=%fused_computation.279.clone.1 | output fusion | flops 66584576 | bytes 4194304 | tf_op jit(solution)/shard_map/reduce-window.50
  564.2 23.2 %fusion.180 = f32[8,256,2,128]{1,0,3,2:T(8,128)S(1)} fusion(f32[8,256,2,128]{1,0,3,2:T(8,128)S(1)} %get-tuple-element.435), kind=kOutput, calls=%fused_computation.41.clone.1 | output fusion | flops 67633152 | bytes 4194304 | tf_op jit(solution)/shard_map/reduce-window.54
  643.0 97.1 %fusion.184 = f32[8,256,2,128]{1,0,3,2:T(8,128)S(1)} fusion(f32[8,256,2,128]{1,0,3,2:T(8,128)S(1)} %get-tuple-element.435), kind=kOutput, calls=%fused_computation.279.clone.1 | output fusion | flops 66584576 | bytes 4194304 | tf_op jit(solution)/shard_map/reduce-window.50
  740.9 23.2 %fusion.180 = f32[8,256,2,128]{1,0,3,2:T(8,128)S(1)} fusion(f32[8,256,2,128]{1,0,3,2:T(8,128)S(1)} %get-tuple-element.435), kind=kOutput, calls=%fused_computation.41.clone.1 | output fusion | flops 67633152 | bytes 4194304 | tf_op jit(solution)/shard_map/reduce-window.54
  819.7 97.1 %fusion.184 = f32[8,256,2,128]{1,0,3,2:T(8,128)S(1)} fusion(f32[8,256,2,128]{1,0,3,2:T(8,128)S(1)} %get-tuple-element.435), kind=kOutput, calls=%fused_computation.279.clone.1 | output fusion | flops 66584576 | bytes 4194304 | tf_op jit(solution)/shard_map/reduce-window.50
  917.6 23.2 %fusion.180 = f32[8,256,2,128]{1,0,3,2:T(8,128)S(1)} fusion(f32[8,256,2,128]{1,0,3,2:T(8,128)S(1)} %get-tuple-element.435), kind=kOutput, calls=%fused_computation.41.clone.1 | output fusion | flops 67633152 | bytes 4194304 | tf_op jit(solution)/shard_map/reduce-window.54
  996.7 8.9 pad_maximum_fusion.1
  1005.5 29.9 %gather_fusion.4 = f32[8192,62]{1,0:T(8,128)} fusion(f32[62,8192]{0,1:T(8,128)} %pad_maximum_fusion.1, s32[8192]{0:T(1024)S(1)} %copy-done.28), kind=kCustom, calls=%fused_computation.4 | custom fusion | bytes 4096000 | tf_op jit(solution)/shard_map/gather | solution.py:150
  1035.4 8.0 reshape.901
  1049.7 28.9 %all-to-all-done.2 = f32[128,1,3968]{2,1,0:T(1,128)} async-done(((f32[128,1,3968]{2,1,0:T(1,128)}), f32[128,1,3968]{2,1,0:T(1,128)}, u32[]{:S(2)}, u32[]{:S(2)}) %all-to-all-start.2) | async-done | bytes 2031648 | tf_op jit(solution)/shard_map/all_to_all | solution.py:151
  1101.8 44.8 %scatter_custom_fusion.1 = f32[11,4096]{0,1:T(8,128)S(1)} fusion(s32[8192]{0:T(1024)} %bitcast.339, f32[8192,11]{1,0:T(8,128)} %bitcast.297, f32[]{:T(128)} %constant.237.clone.1), kind=kCustom, calls=%fused_computation.166 | custom fusion | flops 90112 | bytes 180736 | tf_op jit(solution)/shard_map/scatter-add | solution.py:155
  1147.9 45.0 %scatter_custom_fusion.2 = f32[3,4096]{0,1:T(8,128)S(1)} fusion(s32[8192]{0:T(1024)} %bitcast.340, f32[8192,3]{1,0:T(8,128)} %bitcast.316, f32[]{:T(128)} %constant.237.clone.1), kind=kCustom, calls=%fused_computation.164 | custom fusion | flops 24576 | bytes 49664 | tf_op jit(solution)/shard_map/scatter-add | solution.py:156
  1194.2 44.8 %scatter_custom_fusion.3 = f32[48,4096]{0,1:T(8,128)S(1)} fusion(s32[8192]{0:T(1024)} %bitcast.341, f32[8192,48]{1,0:T(8,128)} %bitcast.315, f32[]{:T(128)} %constant.237.clone.1), kind=kCustom, calls=%fused_computation.162 | custom fusion | flops 393216 | bytes 786944 | tf_op jit(solution)/shard_map/scatter-add | solution.py:157
  (452 shorter events, 340.8 us)
Async XLA Ops:
  8.2 45.6 %copy-start.27 = (s32[8192]{0:T(1024)}, s32[8192]{0:T(1024)S(1)}, u32[]{:S(2)}) copy-start(s32[8192]{0:T(1024)S(1)} %get-tuple-element.305) | copy-start | bytes 98308
  8.3 57.8 %copy-start.29 = (f32[11,4096]{1,0:T(8,128)S(1)}, f32[11,4096]{1,0:T(8,128)}, u32[]{:S(2)}) copy-start(f32[11,4096]{1,0:T(8,128)} %param.10) | copy-start | bytes 540676
  53.8 14.2 %copy-start.36 = (f32[3,4096]{1,0:T(4,128)S(1)}, f32[3,4096]{1,0:T(4,128)}, u32[]{:S(2)}) copy-start(f32[3,4096]{1,0:T(4,128)} %param.11) | copy-start | bytes 147460
  54.5 21.0 %all-to-all-start = ((s32[128,64,1]{1,2,0:T(1,128)}), s32[128,64,1]{1,2,0:T(1,128)S(1)}, u32[]{:S(2)}, u32[]{:S(2)}) async-start(s32[128,64,1]{1,2,0:T(1,128)} %bitcast.30), calls=%async_computation | async-start | bytes 131072 | tf_op jit(solution)/shard_map/all_to_all | solution.py:140
  66.1 4.0 copy-start.23
  77.0 29.3 %copy-start.30 = (s32[8192,1]{0,1:T(1,128)}, s32[8192,1]{0,1:T(1,128)S(1)}, u32[]{:S(2)}) copy-start(s32[8192,1]{0,1:T(1,128)S(1)} %compare_select_fusion.1) | copy-start | bytes 98308
  180.2 5.2 copy-start.38
  180.2 5.8 copy-start.34
  180.2 5.8 copy-start.35
  180.2 5.9 copy-start.37
  180.2 34.9 %all-to-all-start.1 = ((f32[128,1,3968]{2,1,0:T(1,128)}), f32[128,1,3968]{2,1,0:T(1,128)S(1)}, u32[]{:S(2)}, u32[]{:S(2)}) async-start(f32[128,1,3968]{2,1,0:T(1,128)} %reshape.899), calls=%async_computation.1 | async-start | bytes 4063232 | tf_op jit(solution)/shard_map/all_to_all | solution.py:143
  255.0 5.5 copy-start.4
  272.3 3.5 copy-start.25
  282.7 143.4 %copy-start = (f32[8,256,2,128]{1,3,2,0:T(8,128)}, f32[8,256,2,128]{1,3,2,0:T(8,128)S(1)}, u32[]{:S(2)}) copy-start(f32[8,256,2,128]{1,3,2,0:T(8,128)S(1)} %copy.351) | copy-start | bytes 6291460 | tf_op jit(solution)/shard_map/while
  387.5 23.3 %slice-start = ((f32[8,256,3]{1,0,2:T(8,128)}), f32[8,256,2]{1,0,2:T(8,128)S(1)}, s32[]{:S(2)}) async-start(f32[8,256,3]{1,0,2:T(8,128)} %copy-done.11), calls=%async_computation.3 | async-start | bytes 32768 | tf_op jit(solution)/shard_map/slice.113
  459.4 143.4 %copy-start = (f32[8,256,2,128]{1,3,2,0:T(8,128)}, f32[8,256,2,128]{1,3,2,0:T(8,128)S(1)}, u32[]{:S(2)}) copy-start(f32[8,256,2,128]{1,3,2,0:T(8,128)S(1)} %copy.351) | copy-start | bytes 6291460 | tf_op jit(solution)/shard_map/while
  564.2 23.3 %slice-start = ((f32[8,256,3]{1,0,2:T(8,128)}), f32[8,256,2]{1,0,2:T(8,128)S(1)}, s32[]{:S(2)}) async-start(f32[8,256,3]{1,0,2:T(8,128)} %copy-done.11), calls=%async_computation.3 | async-start | bytes 32768 | tf_op jit(solution)/shard_map/slice.113
  636.1 143.4 %copy-start = (f32[8,256,2,128]{1,3,2,0:T(8,128)}, f32[8,256,2,128]{1,3,2,0:T(8,128)S(1)}, u32[]{:S(2)}) copy-start(f32[8,256,2,128]{1,3,2,0:T(8,128)S(1)} %copy.351) | copy-start | bytes 6291460 | tf_op jit(solution)/shard_map/while
  740.9 23.3 %slice-start = ((f32[8,256,3]{1,0,2:T(8,128)}), f32[8,256,2]{1,0,2:T(8,128)S(1)}, s32[]{:S(2)}) async-start(f32[8,256,3]{1,0,2:T(8,128)} %copy-done.11), calls=%async_computation.3 | async-start | bytes 32768 | tf_op jit(solution)/shard_map/slice.113
  812.8 143.4 %copy-start = (f32[8,256,2,128]{1,3,2,0:T(8,128)}, f32[8,256,2,128]{1,3,2,0:T(8,128)S(1)}, u32[]{:S(2)}) copy-start(f32[8,256,2,128]{1,3,2,0:T(8,128)S(1)} %copy.351) | copy-start | bytes 6291460 | tf_op jit(solution)/shard_map/while
  917.6 23.3 %slice-start = ((f32[8,256,3]{1,0,2:T(8,128)}), f32[8,256,2]{1,0,2:T(8,128)S(1)}, s32[]{:S(2)}) async-start(f32[8,256,3]{1,0,2:T(8,128)} %copy-done.11), calls=%async_computation.3 | async-start | bytes 32768 | tf_op jit(solution)/shard_map/slice.113
  996.7 8.9 copy-start.28
  1043.4 35.2 %all-to-all-start.2 = ((f32[128,1,3968]{2,1,0:T(1,128)}), f32[128,1,3968]{2,1,0:T(1,128)}, u32[]{:S(2)}, u32[]{:S(2)}) async-start(f32[128,1,3968]{2,1,0:T(1,128)} %reshape.901), calls=%async_computation.2 | async-start | bytes 4063232 | tf_op jit(solution)/shard_map/all_to_all | solution.py:151
  1093.2 5.4 copy-start.7
  (43 other events, 81.7 us)
where the time goes:
time: 1250 us; the launch traced here: 1240 us
  other arithmetic  776 us (62%)
  local copies, waits for them, and re-layouts  310 us (25%)
  matrix products  66.1 us (5%)
  waiting for transfers between devices  62.7 us (5%)
  starting transfers between devices  22.4 us (2%)
    another operation x56, other arithmetic  533 us
    unnamed x78, local copies, waits for them, and re-layouts  46 us
    gather x1, local copies, waits for them, and re-layouts, on_device(): wanted = (flat % surf_here)[order]  45.5 us
    scatter-add x1, other arithmetic, on_device(): grad_position = jnp.zeros((3, surf_here), jnp.float32).at[:, got].add(dpos)  45 us
    scatter-add x1, other arithmetic, on_device(): grad_splat = jnp.zeros((11, surf_here), jnp.float32).at[:, got].add(dsplat)  44.8 us
    scatter-add x1, other arithmetic, on_device(): grad_harmonics = jnp.zeros((48, surf_here), jnp.float32).at[:, got].add(dsh)  44.8 us
    dot_general x12, matrix products, tile_loss_of(): jnp.einsum('pk,ck->cp', weight, colors, precision=lax.Precision.HIGHEST)  43.7 us
    gather x1, local copies, waits for them, and re-layouts, on_device(): sent_back = jnp.concatenate([dgeom, slot_pos, slot_sh], axis=0)[:, order]  29.9 us
  transfers between devices with their start and end apart: 3, of which 3 were waited for; matrix products, arithmetic and copies ran while one was open for 0% of the time, Pallas kernels for 0%

commit v1 on v0

v1 whole, which is shorter than its diff:
```python
import functools

import jax
import jax.numpy as jnp
from jax import lax
from jax.experimental import pallas as pl
from jax.experimental.pallas import tpu as pltpu
from jax.sharding import PartitionSpec as P

F32 = jnp.float32
BF16 = jnp.bfloat16
I32 = jnp.int32
MESH = pl.DeviceIdType.MESH
N_DEV = 128
TILES = 32
SURF = 4096
SHARE = 48
LOG2E = 1.4426950408889634

sh_zero = 0.28209479177387814
sh_one = 0.4886025119029199
sh_two = (
    1.0925484305920792,
    -1.0925484305920792,
    0.31539156525252005,
    -1.0925484305920792,
    0.5462742152960396,
)
sh_three = (
    -0.5900435899266435,
    2.890611442640554,
    -0.4570457994644658,
    0.3731763325901154,
    -0.4570457994644658,
    1.445305721320277,
    -0.5900435899266435,
)


def iota(shape, dim):
    return lax.broadcasted_iota(I32, shape, dim)


def dot_nn(a, b):
    return lax.dot_general(a, b, (((1,), (0,)), ((), ())), preferred_element_type=F32)


def dot_nt(a, b):
    return lax.dot_general(a, b, (((1,), (1,)), ((), ())), preferred_element_type=F32)


def dot_tn(a, b):
    return lax.dot_general(a, b, (((0,), (0,)), ((), ())), preferred_element_type=F32)


def split2(x):
    hi = x.astype(BF16)
    return hi, (x - hi.astype(F32)).astype(BF16)


def split3(x):
    hi = x.astype(BF16)
    rest = x - hi.astype(F32)
    mid = rest.astype(BF16)
    return hi, mid, (rest - mid.astype(F32)).astype(BF16)


def one_hot_rows(rows, index):
    return jnp.where(iota((rows, index.shape[1]), 0) == index, 1.0, 0.0).astype(BF16)


def directions(pos_rows, cams):
    offs = [pos_rows[d] - cams[:, d : d + 1] for d in range(3)]
    length = jnp.sqrt(offs[0] * offs[0] + offs[1] * offs[1] + offs[2] * offs[2])
    return [o / length for o in offs], length


def sh_basis(x, y, z):
    xx, yy, zz = x * x, y * y, z * z
    t, h = sh_two, sh_three
    return [
        jnp.full_like(x, sh_zero),
        -sh_one * y,
        sh_one * z,
        -sh_one * x,
        t[0] * (x * y),
        t[1] * (y * z),
        t[2] * (2.0 * zz - xx - yy),
        t[3] * (x * z),
        t[4] * (xx - yy),
        h[0] * (y * (3.0 * xx - yy)),
        h[1] * (x * y * z),
        h[2] * (y * (4.0 * zz - xx - yy)),
        h[3] * (z * (2.0 * zz - 3.0 * xx - 3.0 * yy)),
        h[4] * (x * (4.0 * zz - xx - yy)),
        h[5] * (z * (xx - yy)),
        h[6] * (x * (xx - 3.0 * yy)),
    ]


def sh_basis_back(x, y, z, d):
    xx, yy, zz = x * x, y * y, z * z
    xy, yz, xz = x * y, y * z, x * z
    t, h = sh_two, sh_three
    gx = (
        -sh_one * d[3] + t[0] * (y * d[4]) - (2.0 * t[2]) * (x * d[6]) + t[3] * (z * d[7])
        + (2.0 * t[4]) * (x * d[8]) + (6.0 * h[0]) * (xy * d[9]) + h[1] * (yz * d[10])
        - (2.0 * h[2]) * (xy * d[11]) - (6.0 * h[3]) * (xz * d[12])
        + h[4] * ((4.0 * zz - 3.0 * xx - yy) * d[13]) + (2.0 * h[5]) * (xz * d[14])
        + (3.0 * h[6]) * ((xx - yy) * d[15])
    )
    gy = (
        -sh_one * d[1] + t[0] * (x * d[4]) + t[1] * (z * d[5]) - (2.0 * t[2]) * (y * d[6])
        - (2.0 * t[4]) * (y * d[8]) + (3.0 * h[0]) * ((xx - yy) * d[9]) + h[1] * (xz * d[10])
        + h[2] * ((4.0 * zz - xx - 3.0 * yy) * d[11]) - (6.0 * h[3]) * (yz * d[12])
        - (2.0 * h[4]) * (xy * d[13]) - (2.0 * h[5]) * (yz * d[14]) - (6.0 * h[6]) * (xy * d[15])
    )
    gz = (
        sh_one * d[2] + t[1] * (y * d[5]) + (4.0 * t[2]) * (z * d[6]) + t[3] * (x * d[7])
        + h[1] * (xy * d[10]) + (8.0 * h[2]) * (yz * d[11])
        + h[3] * ((6.0 * zz - 3.0 * xx - 3.0 * yy) * d[12]) + (8.0 * h[4]) * (xz * d[13])
        + h[5] * ((xx - yy) * d[14])
    )
    return gx, gy, gz


def route_kernel(lists_ref, counts_ref, send_ref, pos_ref, upper):
    upper[...] = jnp.where(iota((256, 256), 0) < iota((256, 256), 1), 1.0, 0.0).astype(BF16)
    holder_id = iota((N_DEV, 256), 0)
    lane = iota((1, 256), 1)

    def tile(t, state):
        carry, acc_hi, acc_lo = state
        flat = lists_ref[pl.ds(t, 1), :]
        live = lane < counts_ref[t]
        holder = jnp.where(live, flat // SURF, -1)
        local = flat % SURF
        mine = holder_id == holder
        ones = jnp.where(mine, 1.0, 0.0)
        count = dot_nn(ones.astype(BF16), upper[...]) + carry
        rank = jnp.sum(ones * count, axis=0, keepdims=True).astype(I32)
        pos_ref[pl.ds(t, 1), :] = jnp.where(live, holder * 64 + rank, -1)
        hi = jnp.where(mine, (local // 64).astype(F32), 0.0).astype(BF16)
        lo = jnp.where(mine, (local % 64).astype(F32), 0.0).astype(BF16)
        rank_hot = jnp.where((iota((N_DEV, 256), 0) & 63) == rank, 1.0, 0.0).astype(BF16)
        carry = carry + jnp.sum(ones, axis=1, keepdims=True)
        return carry, acc_hi + dot_nt(hi, rank_hot), acc_lo + dot_nt(lo, rank_hot)

    zero = jnp.zeros((N_DEV, 128), F32)
    _, acc_hi, acc_lo = lax.fori_loop(0, TILES, tile, (jnp.zeros((N_DEV, 1), F32), zero, zero))
    local = (acc_hi * 64.0 + acc_lo).astype(I32)
    send_ref[:, 0, :] = jnp.where((iota((N_DEV, 128), 1) & 63) < SHARE, local, -1)


def exchange_kernel(x_ref, o_ref, send_sem, recv_sem, own_sem):
    me = lax.axis_index("surf")
    barrier = pltpu.get_barrier_semaphore()

    def greet(i, c):
        pl.semaphore_signal(
            barrier, inc=1, device_id=(lax.rem(me + i, N_DEV),), device_id_type=MESH
        )
        return c

    lax.fori_loop(1, N_DEV, greet, 0)
    own = pltpu.make_async_copy(x_ref.at[me], o_ref.at[me], own_sem)
    own.start()
    pl.semaphore_wait(barrier, N_DEV - 1)

    def send(i, c):
        peer = lax.rem(me + i, N_DEV)
        pltpu.make_async_remote_copy(
            src_ref=x_ref.at[peer],
            dst_ref=o_ref.at[me],
            send_sem=send_sem,
            recv_sem=recv_sem,
            device_id=(peer,),
            device_id_type=MESH,
        ).start()
        return c

    lax.fori_loop(1, N_DEV, send, 0)
    own.wait()
    pltpu.make_async_remote_copy(
        src_ref=x_ref.at[pl.ds(0, N_DEV - 1)],
        dst_ref=o_ref.at[pl.ds(0, N_DEV - 1)],
        send_sem=send_sem,
        recv_sem=recv_sem,
        device_id=(me,),
        device_id_type=MESH,
    ).wait()


def pair_lanes(even, odd):
    return jnp.where(iota(even.shape, 1) < 64, even, odd)


def fetch_index(got_ref, q):
    rows = [got_ref[4 * q + i] for i in range(4)]
    return jnp.concatenate([pair_lanes(rows[0], rows[1]), pair_lanes(rows[2], rows[3])], axis=1)


def pack_pair(g, out_ref, first):
    top, low = g[0:8], g[8:16]
    out_ref[first] = pair_lanes(top, pltpu.roll(low, 64, 1))
    out_ref[first + 1] = pair_lanes(pltpu.roll(top, 64, 1), low)


def unpack_pair(in_ref, first):
    even, odd = in_ref[first], in_ref[first + 1]
    return jnp.concatenate(
        [pair_lanes(even, pltpu.roll(odd, 64, 1)), pair_lanes(pltpu.roll(even, 64, 1), odd)], axis=0
    )


def gather_kernel(splat_ref, position_ref, harmonics_ref, cams_ref, got_ref, out_ref, table):
    cams = cams_ref[...]

    def build(h, c):
        lanes = pl.ds(pl.multiple_of(h * 256, 256), 256)
        (x, y, z), _ = directions([position_ref[d : d + 1, lanes] for d in range(3)], cams)
        basis = sh_basis(x, y, z)
        colors = []
        for ch in range(3):
            total = jnp.zeros_like(x)
            for b in range(16):
                total = total + harmonics_ref[ch * 16 + b : ch * 16 + b + 1, lanes] * basis[b]
            colors.append(jnp.maximum(total + 0.5, 0.0))
        splat = splat_ref[:, lanes]
        for v in range(4):
            rows = jnp.concatenate(
                [splat] + [col[v : v + 1] for col in colors] + [jnp.zeros((2, 256), F32)], axis=0
            )
            table[v, pl.ds(pl.multiple_of(h * 16, 16), 16), :] = jnp.concatenate(split3(rows), axis=1)
        return c

    lax.fori_loop(0, 16, build, 0)

    def fetch(q, c):
        index = fetch_index(got_ref, q)
        hot = one_hot_rows(256, index & 255)
        found = dot_nn(table[q // 8], jnp.concatenate([hot, hot, hot], axis=0))
        high = index >> 8
        g = jnp.zeros((16, 256), F32)
        for h in range(16):
            g = g + jnp.where(high == h, found[h * 16 : h * 16 + 16], 0.0)
        pack_pair(g[:, 0:128], out_ref, 4 * q)
        pack_pair(g[:, 128:256], out_ref, 4 * q + 2)
        return c

    lax.fori_loop(0, 32, fetch, 0)


def tiles_kernel(
    recv_ref, pos_ref, counts_ref, color_ref, normal_ref, loss_ref, out_ref,
    table, acc, before, sign, after, mono_col, mono_row,
):
    for q in range(32):
        for half in range(2):
            g = unpack_pair(recv_ref, 4 * q + 2 * half)
            for s, part in enumerate(split3(g)):
                table[q * 16 : q * 16 + 16, s * 256 + half * 128 : s * 256 + half * 128 + 128] = part
    acc[...] = jnp.zeros_like(acc)
    j, k = iota((512, 256), 0) & 255, iota((512, 256), 1)
    before[...] = jnp.where(j < k, 1.0, 0.0).astype(BF16)
    sign[...] = jnp.where(j < k, 1.0, jnp.where(j > k, -1.0, 0.0)).astype(BF16)
    after[...] = jnp.where(j > k, 1.0, 0.0).astype(BF16)

    def monomials(pixel, which):
        px = ((pixel & 15).astype(F32) - 7.5) * 0.125
        py = ((pixel >> 4).astype(F32) - 7.5) * 0.125
        m = jnp.where(which == 0, 1.0, 0.0)
        for n, value in ((1, px), (2, py), (3, px * px), (4, px * py), (5, py * py)):
            m = jnp.where(which == n, value, m)
        return m

    col = iota((256, 128), 1)
    mono_col[...] = jnp.where(
        col < 24, monomials(iota((256, 128), 0), col & 7), 0.0
    ).astype(BF16)
    mono_row[...] = monomials(iota((16, 512), 1) & 255, iota((16, 512), 0)).astype(BF16)

    lane = iota((1, 256), 1)
    row8 = iota((8, 256), 0)
    y_scale = jnp.where(row8 < 3, -0.25, jnp.where(row8 < 6, 1.0, 0.0))
    y_const = jnp.where(row8 == 6, 0.25, 0.0)
    zero1 = jnp.zeros((1, 256), F32)
    zero8 = jnp.zeros((8, 256), F32)
    kappa = 2.0 / 256.0

    def tile(t, c):
        index = pos_ref[pl.ds(t, 1), :]
        live = lane < counts_ref[t]
        high = index >> 8
        hot = one_hot_rows(256, index & 255)
        found = dot_nn(table[...], jnp.concatenate([hot, hot, hot], axis=0))
        g = jnp.zeros((16, 256), F32)
        for h in range(32):
            g = g + jnp.where(high == h, found[h * 16 : h * 16 + 16], 0.0)
        a0, a1, a2, b0, b1, b2, logit, depth = [g[r : r + 1] for r in range(8)]
        v8 = g[8:16]

        s = -0.5 * LOG2E
        grow = jnp.exp(-logit)
        offset = jnp.log(1.0 + grow) * (-LOG2E) + (-0.07400058144377693)
        sig = 1.0 / (1.0 + grow)
        c0 = jnp.where(live, s * (a0 * a0 + b0 * b0) + offset, -1e4)
        coef = jnp.concatenate(
            [
                c0,
                (2.0 * s) * (a0 * a1 + b0 * b1),
                (2.0 * s) * (a0 * a2 + b0 * b2),
                s * (a1 * a1 + b1 * b1),
                (2.0 * s) * (a1 * a2 + b1 * b2),
                s * (a2 * a2 + b2 * b2),
                zero1,
                zero1,
            ],
            axis=0,
        )
        coef = jnp.concatenate([p.astype(F32) for p in split3(coef)] + [zero8], axis=0).astype(BF16)
        alpha = jnp.exp2(dot_nn(mono_col[:, 0:32], coef))
        logkeep = jnp.log(1.0 - alpha)
        trans = jnp.exp(dot_nn(jnp.concatenate(split2(logkeep), axis=1), before[...]))
        w = alpha * trans
        wh, wl = split2(w)
        w2 = jnp.concatenate([wh, wl], axis=1)
        am = dot_nn(w2, sign[...])
        bm = dot_nn(jnp.concatenate(split2(w * depth), axis=1), sign[...])

        vh, vl = split2(v8)
        v16 = jnp.concatenate([vh.astype(F32), vl.astype(F32)], axis=0).astype(BF16)
        shown = dot_nt(jnp.concatenate([v16, v16], axis=1), w2)
        shown = shown[0:8] + shown[8:16]
        resid = shown[3:6] - color_ref[:, t, :]
        x8 = jnp.concatenate([normal_ref[:, t, :], resid, zero1 + 1.0, zero1], axis=0)
        y8 = v8 * y_scale + y_const
        xh, xl = [p.astype(F32) for p in split2(x8)]
        yh, yl = [p.astype(F32) for p in split2(y8)]
        x32 = jnp.concatenate([xh, xl, xh, zero8], axis=0).astype(BF16)
        y32 = jnp.concatenate([yh, yh, yl, zero8], axis=0).astype(BF16)
        grad_w = dot_tn(x32, y32) + (depth * am - bm)
        y = grad_w * w
        behind = dot_nn(jnp.concatenate(split2(y), axis=1), after[...])
        hgrad = y - behind * (alpha * jnp.exp(-logkeep))

        moments = dot_nn(mono_row[...], jnp.concatenate(split2(hgrad), axis=0))
        x16 = x32[0:16]
        dv = dot_nn(jnp.concatenate([x16, x16], axis=1), jnp.concatenate([wh, wl], axis=0))
        dv = dv[0:8] + dv[8:16]
        ga = jnp.sum(w * am, axis=0, keepdims=True)
        m0, m1, m2, m3, m4, m5 = [moments[r : r + 1] * (-kappa) for r in range(6)]

        out = jnp.concatenate(
            [
                a0 * m0 + a1 * m1 + a2 * m2,
                a0 * m1 + a1 * m3 + a2 * m4,
                a0 * m2 + a1 * m4 + a2 * m5,
                b0 * m0 + b1 * m1 + b2 * m2,
                b0 * m1 + b1 * m3 + b2 * m4,
                b0 * m2 + b1 * m4 + b2 * m5,
                (sig - 1.0) * m0,
                kappa * ga,
                dv * jnp.where(row8 < 3, -0.25 * kappa, jnp.where(row8 < 6, kappa, 0.0)),
            ],
            axis=0,
        )
        color_sum = jnp.sum(resid * resid)
        slot_sum = jnp.sum(
            2.0 * (depth * ga)
            + 0.5 * (dv[6:7] - v8[0:1] * dv[0:1] - v8[1:2] * dv[1:2] - v8[2:3] * dv[2:3])
        )
        loss_ref[pl.ds(t, 1), :] = jnp.full((1, 128), (color_sum + slot_sum) * (1.0 / 256.0), F32)

        oh, ol = [p.astype(F32) for p in split2(out)]
        both = jnp.concatenate([oh, ol], axis=1)
        high2 = jnp.concatenate([high, high], axis=1)
        spread = jnp.concatenate(
            [jnp.where(high2 == h, both, 0.0).astype(BF16) for h in range(32)], axis=0
        )
        acc[...] += dot_nt(spread, jnp.concatenate([hot, hot], axis=1))
        return c

    lax.fori_loop(0, TILES, tile, 0)
    for q in range(32):
        for half in range(2):
            pack_pair(
                acc[q * 16 : q * 16 + 16, half * 128 : half * 128 + 128], out_ref, 4 * q + 2 * half
            )


def surfel_kernel(
    back_ref, got_ref, position_ref, harmonics_ref, cams_ref, gs_ref, gp_ref, gh_ref, acc
):
    acc[...] = jnp.zeros_like(acc)

    def add(q, c):
        index = fetch_index(got_ref, q)
        hot = one_hot_rows(256, index & 255)
        high = index >> 8
        d = jnp.concatenate([unpack_pair(back_ref, 4 * q), unpack_pair(back_ref, 4 * q + 2)], axis=1)
        dh, dl = [p.astype(F32) for p in split2(d)]
        both = jnp.concatenate([dh, dl], axis=1)
        high2 = jnp.concatenate([high, high], axis=1)
        spread = jnp.concatenate(
            [jnp.where(high2 == h, both, 0.0).astype(BF16) for h in range(16)], axis=0
        )
        acc[q // 8] += dot_nt(spread, jnp.concatenate([hot, hot], axis=1))
        return c

    lax.fori_loop(0, 32, add, 0)
    cams = cams_ref[...]

    def finish(h, c):
        lanes = pl.ds(pl.multiple_of(h * 256, 256), 256)
        views = [acc[v, pl.ds(pl.multiple_of(h * 16, 16), 16), :] for v in range(4)]
        total = (views[0] + views[1]) + (views[2] + views[3])
        gs_ref[:, lanes] = total[0:11]
        dirs, length = directions([position_ref[d : d + 1, lanes] for d in range(3)], cams)
        x, y, z = dirs
        basis = sh_basis(x, y, z)
        dbasis = [jnp.zeros_like(x) for _ in range(16)]
        for ch in range(3):
            coeffs = [harmonics_ref[ch * 16 + b : ch * 16 + b + 1, lanes] for b in range(16)]
            value = jnp.zeros_like(x)
            for b in range(16):
                value = value + coeffs[b] * basis[b]
            value = value + 0.5
            dcol = jnp.concatenate([views[v][11 + ch : 12 + ch] for v in range(4)], axis=0)
            dcol = dcol * jnp.where(value > 0.0, 1.0, jnp.where(value == 0.0, 0.5, 0.0))
            for b in range(16):
                gh_ref[ch * 16 + b : ch * 16 + b + 1, lanes] = jnp.sum(
                    dcol * basis[b], axis=0, keepdims=True
                )
                dbasis[b] = dbasis[b] + dcol * coeffs[b]
        grads = sh_basis_back(x, y, z, dbasis)
        along = grads[0] * x + grads[1] * y + grads[2] * z
        for d in range(3):
            gp_ref[d : d + 1, lanes] = jnp.sum(
                (grads[d] - dirs[d] * along) / length, axis=0, keepdims=True
            )
        return c

    lax.fori_loop(0, 16, finish, 0)


VM = pl.BlockSpec(memory_space=pltpu.VMEM)
SM = pl.BlockSpec(memory_space=pltpu.SMEM)
LIMIT = 48 * 1024 * 1024


def exchange(x, collective_id, name):
    return pl.pallas_call(
        exchange_kernel,
        out_shape=jax.ShapeDtypeStruct(x.shape, x.dtype),
        in_specs=[VM],
        out_specs=VM,
        scratch_shapes=[pltpu.SemaphoreType.DMA] * 3,
        compiler_params=pltpu.CompilerParams(collective_id=collective_id, has_side_effects=True),
        name=name,
    )(x)


def local_call(kernel, out_shape, in_specs, scratch, name):
    outs = tuple(jax.ShapeDtypeStruct(s, d) for s, d in out_shape)
    return pl.pallas_call(
        kernel,
        out_shape=outs,
        in_specs=in_specs,
        out_specs=tuple(VM for _ in outs),
        scratch_shapes=scratch,
        compiler_params=pltpu.CompilerParams(vmem_limit_bytes=LIMIT),
        name=name,
    )


def on_device(
    splat, position, harmonics, cameras, tile_lists, tile_counts, target_color, target_normal
):
    send, pos = local_call(
        route_kernel,
        [((N_DEV, 1, 128), I32), ((TILES, 256), I32)],
        [VM, SM],
        [pltpu.VMEM((256, 256), BF16)],
        "route",
    )(tile_lists, tile_counts)
    got = exchange(send, 0, "exchange_requests")
    (rows,) = local_call(
        gather_kernel,
        [((N_DEV, 8, 128), F32)],
        [VM] * 5,
        [pltpu.VMEM((4, 256, 768), BF16)],
        "gather_rows",
    )(splat, position, harmonics, cameras, got)
    recv = exchange(rows, 1, "exchange_rows")
    loss, grads = local_call(
        tiles_kernel,
        [((TILES, 128), F32), ((N_DEV, 8, 128), F32)],
        [VM, VM, SM, VM, VM],
        [
            pltpu.VMEM((512, 768), BF16),
            pltpu.VMEM((512, 256), F32),
            pltpu.VMEM((512, 256), BF16),
            pltpu.VMEM((512, 256), BF16),
            pltpu.VMEM((512, 256), BF16),
            pltpu.VMEM((256, 128), BF16),
            pltpu.VMEM((16, 512), BF16),
        ],
        "composite_tiles",
    )(recv, pos, tile_counts, target_color, target_normal)
    back = exchange(grads, 1, "exchange_grads")
    gs, gp, gh = local_call(
        surfel_kernel,
        [((11, SURF), F32), ((3, SURF), F32), ((48, SURF), F32)],
        [VM] * 5,
        [pltpu.VMEM((4, 256, 256), F32)],
        "surfel_grads",
    )(back, got, position, harmonics, cameras)
    return gs, gp, gh, loss[:, 0]


def solution(mesh):
    return jax.shard_map(
        on_device,
        mesh=mesh,
        in_specs=(
            P(None, "surf"),
            P(None, "surf"),
            P(None, "surf"),
            P(),
            P("surf", None),
            P("surf"),
            P(None, "surf", None),
            P(None, "surf", None),
        ),
        out_specs=(P(None, "surf"), P(None, "surf"), P(None, "surf"), P("surf")),
        check_vma=False,
    )
```

time: 1250 us -> 172 us (0.14)
  other arithmetic: 776 us -> 0 us
  local copies, waits for them, and re-layouts: 310 us -> 9.26 us
  Pallas kernels: 0 us -> 161 us
  matrix products: 66.1 us -> 0 us
  waiting for transfers between devices: 62.7 us -> 0 us
  starting transfers between devices: 22.4 us -> 0 us
    another operation x57 -> x0, other arithmetic: 534 us -> none
    gather x5 -> x0, local copies, waits for them, and re-layouts: 162 us -> none  [the longest x1 45.5 us: on_device(): wanted = (flat % surf_here)[order]]
    pallas_call x0 -> x7, Pallas kernels: none -> 161 us  [the longest x1 68.4 us: on_device(): local_call(tiles_kernel, [((TILES, 128), F32), ((N_DEV, 8, 128), F32)], [...]
    scatter-add x3 -> x0, other arithmetic: 135 us -> none  [the longest x1 45 us: on_device(): grad_position = jnp.zeros((3, surf_here), jnp.float32).at[:, got].add(dpos)]
    dot_general x20 -> x0, matrix products: 66.1 us -> none  [the longest x12 43.7 us: tile_loss_of(): jnp.einsum('pk,ck->cp', weight, colors, precision=lax.Precision.HIGHEST)]
    all_to_all x3 -> x0, waiting for transfers between devices: 62.7 us -> none  [the longest x1 29 us: on_device(): lax.all_to_all(payload, 'surf', split_axis=1, concat_axis=1, tiled=True)]
    unnamed x78 -> x34, local copies, waits for them, and re-layouts: 46 us -> 8.64 us
    reduce_sum x11 -> x0, other arithmetic: 36.4 us -> none  [the longest x4 19.3 us: tile_loss_of(): geom[2][None, :] * py[:, None]]
  transfers between devices with their start and end apart: 3 -> 0, of which waited for: 3 -> 0; matrix products, arithmetic and copies ran while one was open for 0% -> 0% of each run, Pallas kernels for 0% -> 0%
where the time goes in v1:
time: 172 us; the launch traced here: 171 us
  Pallas kernels  161 us (94%)
  local copies, waits for them, and re-layouts  9.26 us (5%)
    pallas_call x1, Pallas kernels, on_device(): local_call(tiles_kernel, [((TILES, 128), F32), ((N_DEV, 8, 128), F32)], [...  68.4 us
    pallas_call x3, Pallas kernels, exchange(): pl.pallas_call(exchange_kernel, out_shape=jax.ShapeDtypeStruct(x.shape, x...  50.5 us
    pallas_call x1, Pallas kernels, on_device(): local_call(surfel_kernel, [((11, SURF), F32), ((3, SURF), F32), ((48, SUR...  15.3 us
    pallas_call x1, Pallas kernels, on_device(): local_call(gather_kernel, [((N_DEV, 8, 128), F32)], [VM] * 5, [pltpu.VMEM...  13.7 us
    pallas_call x1, Pallas kernels, on_device(): local_call(route_kernel, [((N_DEV, 1, 128), I32), ((TILES, 256), I32)], [...  13.5 us
    unnamed x34, local copies, waits for them, and re-layouts  8.64 us

profile of v1, /device:TPU:1, one launch (start us, length us, event | category | flops | bytes accessed | tf_op | source)
XLA Modules:
  0.0 171.5 jit_solution(17705003979481425595)
XLA Ops:
  0.6 0.0 copy-start.13
  0.6 0.7 copy-done.13
  1.4 0.7 copy-done.15
  2.0 13.5 %route.1 = (s32[128,1,128]{2,1,0:T(1,128)S(1)}, s32[32,256]{1,0:T(8,128)S(1)}) custom-call(s32[32,256]{1,0:T(8,128)S(1)} %copy-done.13, s32[32]{0:T(128)S(1)} %copy-done.15), custom_call_target="tpu_custom_call" | custom-call | tf_op jit(solution)/shard_map/route/pallas_call | solution.py:480
  15.6 0.0 copy-start.12
  15.6 0.6 copy-done.12
  16.2 16.9 %exchange_requests.1.got_ref = s32[128,1,128]{2,1,0:T(1,128)} custom-call(s32[128,1,128]{2,1,0:T(1,128)} %copy-done.12), custom_call_target="tpu_custom_call" | custom-call | tf_op jit(solution)/shard_map/exchange_requests/pallas_call | solution.py:453
  33.1 0.0 copy-done.9
  33.1 0.0 copy-done.14
  33.1 0.0 copy-start
  33.1 1.1 copy-done
  34.2 0.8 copy-done.5
  35.1 0.9 copy-done.8
  36.0 13.7 %gather_rows.1.x_ref = f32[128,8,128]{2,1,0:T(8,128)S(1)} custom-call(f32[11,4096]{1,0:T(8,128)S(1)} %copy-done.8, f32[3,4096]{1,0:T(4,128)S(1)} %copy-done.9, f32[48,4096]{1,0:T(8,128)S(1)} %copy-done, f32[4,3]{1,0:T(4,128)S(1)} %copy-done.14, s32[128,1,128]{2,1,0:T(1,128)S(1)} %copy-done.5), custom_call_target="tpu_custom_call" | custom-call | tf_op jit(solution)/shard_map/gather_rows/pallas_call | solution.py:488
  49.7 0.8 copy-done.4
  50.5 16.7 %exchange_rows.1.recv_ref = f32[128,8,128]{2,1,0:T(8,128)} custom-call(f32[128,8,128]{2,1,0:T(8,128)} %copy-done.4), custom_call_target="tpu_custom_call" | custom-call | tf_op jit(solution)/shard_map/exchange_rows/pallas_call | solution.py:453
  67.3 1.0 copy-done.3
  68.3 68.4 %composite_tiles.1 = (f32[32,128]{1,0:T(8,128)S(1)}, f32[128,8,128]{2,1,0:T(8,128)S(1)}) custom-call(f32[128,8,128]{2,1,0:T(8,128)S(1)} %copy-done.3, s32[32,256]{1,0:T(8,128)S(1)} %get-tuple-element.12.pos_ref, s32[32]{0:T(128)S(1)} %copy-done.16, f32[3,32,256]{2,1,0:T(8,128)S(1)} %copy-done.10, f32[3,32,256]{2,1,0:T(8,128)S(1)} %copy-done.11), custom_call_target="tpu_custom_call" | custom-call | tf_op jit(solution)/shard_map/composite_tiles/pallas_call | solution.py:496
  136.8 0.0 copy-start.7
  136.8 0.8 copy-done.7
  137.6 16.9 %exchange_grads.1.back_ref = f32[128,8,128]{2,1,0:T(8,128)} custom-call(f32[128,8,128]{2,1,0:T(8,128)} %copy-done.7), custom_call_target="tpu_custom_call" | custom-call | tf_op jit(solution)/shard_map/exchange_grads/pallas_call | solution.py:453
  154.5 0.6 slice_reduce_fusion
  155.1 1.0 copy-done.2
  156.2 15.3 %surfel_grads.1 = (f32[11,4096]{1,0:T(8,128)}, f32[3,4096]{1,0:T(4,128)}, f32[48,4096]{1,0:T(8,128)}) custom-call(f32[128,8,128]{2,1,0:T(8,128)S(1)} %copy-done.2, s32[128,1,128]{2,1,0:T(1,128)S(1)} %copy-done.6, f32[3,4096]{1,0:T(4,128)S(1)} %copy-done.9, f32[48,4096]{1,0:T(8,128)S(1)} %copy-done.1, f32[4,3]{1,0:T(4,128)S(1)} %copy-done.14), custom_call_target="tpu_custom_call" | custom-call | tf_op jit(solution)/shard_map/surfel_grads/pallas_call | solution.py:512
  (18 shorter events, 0.0 us)
Async XLA Ops:
  0.6 0.8 copy-start.13
  1.4 0.7 copy-start.15
  15.6 0.6 copy-start.12
  16.2 16.9 %copy-start.9 = (f32[3,4096]{1,0:T(4,128)S(1)}, f32[3,4096]{1,0:T(4,128)}, u32[]{:S(2)}) copy-start(f32[3,4096]{1,0:T(4,128)} %position_ref.3) | copy-start | bytes 147460
  16.2 16.9 %copy-start.14 = (f32[4,3]{1,0:T(4,128)S(1)}, f32[4,3]{1,0:T(4,128)}, u32[]{:S(2)}) copy-start(f32[4,3]{1,0:T(4,128)} %cams_ref.3) | copy-start | bytes 148
  33.1 1.1 copy-start
  34.2 0.8 copy-start.5
  35.1 0.9 copy-start.8
  49.7 0.8 copy-start.4
  50.5 16.7 %copy-start.10 = (f32[3,32,256]{2,1,0:T(8,128)S(1)}, f32[3,32,256]{2,1,0:T(8,128)}, u32[]{:S(2)}) copy-start(f32[3,32,256]{2,1,0:T(8,128)} %color_ref.1) | copy-start | bytes 294916
  50.5 16.7 %copy-start.11 = (f32[3,32,256]{2,1,0:T(8,128)S(1)}, f32[3,32,256]{2,1,0:T(8,128)}, u32[]{:S(2)}) copy-start(f32[3,32,256]{2,1,0:T(8,128)} %normal_ref.1) | copy-start | bytes 294916
  50.5 16.7 %copy-start.16 = (s32[32]{0:T(128)S(1)}, s32[32]{0:T(128)}, u32[]{:S(2)}) copy-start(s32[32]{0:T(128)} %counts_ref.3) | copy-start | bytes 388
  67.3 1.0 copy-start.3
  68.3 86.8 %copy-start.1 = (f32[48,4096]{1,0:T(8,128)S(1)}, f32[48,4096]{1,0:T(8,128)}, u32[]{:S(2)}) copy-start(f32[48,4096]{1,0:T(8,128)} %harmonics_ref.3) | copy-start | bytes 2359300
  136.8 0.8 copy-start.7
  137.6 17.5 %copy-start.6 = (s32[128,1,128]{2,1,0:T(1,128)S(1)}, s32[128,1,128]{2,1,0:T(1,128)}, u32[]{:S(2)}) copy-start(s32[128,1,128]{2,1,0:T(1,128)} %exchange_requests.1.got_ref) | copy-start | bytes 196612
  155.1 1.0 copy-start.2

commit v2 on v1

v2 whole, which is shorter than its diff:
```python
import functools

import jax
import jax.numpy as jnp
from jax import lax
from jax.experimental import pallas as pl
from jax.experimental.pallas import tpu as pltpu
from jax.sharding import PartitionSpec as P

F32 = jnp.float32
BF16 = jnp.bfloat16
I32 = jnp.int32
MESH = pl.DeviceIdType.MESH
N_DEV = 128
TILES = 32
SURF = 4096
SHARE = 48
LOG2E = 1.4426950408889634
LOG2_TOP = -0.07400058144377693
GROUP = 4

sh_zero = 0.28209479177387814
sh_one = 0.4886025119029199
sh_two = (
    1.0925484305920792,
    -1.0925484305920792,
    0.31539156525252005,
    -1.0925484305920792,
    0.5462742152960396,
)
sh_three = (
    -0.5900435899266435,
    2.890611442640554,
    -0.4570457994644658,
    0.3731763325901154,
    -0.4570457994644658,
    1.445305721320277,
    -0.5900435899266435,
)


def iota(shape, dim):
    return lax.broadcasted_iota(I32, shape, dim)


def dot_nn(a, b):
    return lax.dot_general(a, b, (((1,), (0,)), ((), ())), preferred_element_type=F32)


def dot_nt(a, b):
    return lax.dot_general(a, b, (((1,), (1,)), ((), ())), preferred_element_type=F32)


def dot_tn(a, b):
    return lax.dot_general(a, b, (((0,), (0,)), ((), ())), preferred_element_type=F32)


def split2(x):
    hi = x.astype(BF16)
    return hi, (x - hi.astype(F32)).astype(BF16)


def split3(x):
    hi = x.astype(BF16)
    rest = x - hi.astype(F32)
    mid = rest.astype(BF16)
    return hi, mid, (rest - mid.astype(F32)).astype(BF16)


def one_hot_rows(rows, index):
    return jnp.where(iota((rows, index.shape[1]), 0) == index, 1.0, 0.0).astype(BF16)


def directions(pos_rows, cams):
    offs = [pos_rows[d] - cams[:, d : d + 1] for d in range(3)]
    length = jnp.sqrt(offs[0] * offs[0] + offs[1] * offs[1] + offs[2] * offs[2])
    return [o / length for o in offs], length


def sh_basis(x, y, z):
    xx, yy, zz = x * x, y * y, z * z
    t, h = sh_two, sh_three
    return [
        jnp.full_like(x, sh_zero),
        -sh_one * y,
        sh_one * z,
        -sh_one * x,
        t[0] * (x * y),
        t[1] * (y * z),
        t[2] * (2.0 * zz - xx - yy),
        t[3] * (x * z),
        t[4] * (xx - yy),
        h[0] * (y * (3.0 * xx - yy)),
        h[1] * (x * y * z),
        h[2] * (y * (4.0 * zz - xx - yy)),
        h[3] * (z * (2.0 * zz - 3.0 * xx - 3.0 * yy)),
        h[4] * (x * (4.0 * zz - xx - yy)),
        h[5] * (z * (xx - yy)),
        h[6] * (x * (xx - 3.0 * yy)),
    ]


def sh_basis_back(x, y, z, d):
    xx, yy, zz = x * x, y * y, z * z
    xy, yz, xz = x * y, y * z, x * z
    t, h = sh_two, sh_three
    gx = (
        -sh_one * d[3] + t[0] * (y * d[4]) - (2.0 * t[2]) * (x * d[6]) + t[3] * (z * d[7])
        + (2.0 * t[4]) * (x * d[8]) + (6.0 * h[0]) * (xy * d[9]) + h[1] * (yz * d[10])
        - (2.0 * h[2]) * (xy * d[11]) - (6.0 * h[3]) * (xz * d[12])
        + h[4] * ((4.0 * zz - 3.0 * xx - yy) * d[13]) + (2.0 * h[5]) * (xz * d[14])
        + (3.0 * h[6]) * ((xx - yy) * d[15])
    )
    gy = (
        -sh_one * d[1] + t[0] * (x * d[4]) + t[1] * (z * d[5]) - (2.0 * t[2]) * (y * d[6])
        - (2.0 * t[4]) * (y * d[8]) + (3.0 * h[0]) * ((xx - yy) * d[9]) + h[1] * (xz * d[10])
        + h[2] * ((4.0 * zz - xx - 3.0 * yy) * d[11]) - (6.0 * h[3]) * (yz * d[12])
        - (2.0 * h[4]) * (xy * d[13]) - (2.0 * h[5]) * (yz * d[14]) - (6.0 * h[6]) * (xy * d[15])
    )
    gz = (
        sh_one * d[2] + t[1] * (y * d[5]) + (4.0 * t[2]) * (z * d[6]) + t[3] * (x * d[7])
        + h[1] * (xy * d[10]) + (8.0 * h[2]) * (yz * d[11])
        + h[3] * ((6.0 * zz - 3.0 * xx - 3.0 * yy) * d[12]) + (8.0 * h[4]) * (xz * d[13])
        + h[5] * ((xx - yy) * d[14])
    )
    return gx, gy, gz


def lane_of(x):
    return iota(x.shape, 1)


def join_eight(pieces):
    blocks = [jnp.zeros_like(pieces[0]) for _ in range(3)]
    for s, piece in enumerate(pieces):
        b, lo = divmod(SHARE * s, 128)
        lane = lane_of(piece)
        blocks[b] = jnp.where((lane >= lo) & (lane < lo + SHARE), piece, blocks[b])
        if lo + SHARE > 128:
            blocks[b + 1] = jnp.where(lane < lo + SHARE - 128, piece, blocks[b + 1])
    return blocks


def split_eight(blocks):
    pieces = []
    for s in range(8):
        b, lo = divmod(SHARE * s, 128)
        piece = pltpu.roll(blocks[b], 128 - lo, 1) if lo else blocks[b]
        if lo + SHARE > 128:
            piece = jnp.where(
                lane_of(piece) < 128 - lo, piece, pltpu.roll(blocks[b + 1], 128 - lo, 1)
            )
        pieces.append(piece)
    return pieces


def shift(x, amount):
    return pltpu.roll(x, amount % 128, 1) if amount % 128 else x


def index_blocks(ref, first):
    return join_eight([shift(ref[first + s], SHARE * s) for s in range(8)])


def message_blocks(ref, first):
    pieces = []
    for s in range(8):
        tile = ref[first + s]
        pieces.append(
            jnp.concatenate([shift(tile, SHARE * s), shift(tile, SHARE * s + 64)], axis=0)
        )
    return join_eight(pieces)


def write_messages(ref, first, blocks):
    for s, piece in enumerate(split_eight(blocks)):
        ref[first + s] = jnp.where(
            lane_of(piece[0:8]) < 64, piece[0:8], pltpu.roll(piece[8:16], 64, 1)
        )


def wide(blocks):
    return [
        jnp.concatenate(blocks[2 * i : 2 * i + 2], axis=1) for i in range(len(blocks) // 2)
    ]


def halves(chunks):
    return [c[:, 128 * i : 128 * i + 128] for c in chunks for i in range(2)]


def pick_rows(found, high, count):
    parts = [jnp.where(high == h, found[h * 16 : h * 16 + 16], 0.0) for h in range(count)]
    while len(parts) > 1:
        pairs = [parts[i] + parts[i + 1] for i in range(0, len(parts) - 1, 2)]
        parts = pairs + ([parts[-1]] if len(parts) % 2 else [])
    return parts[0]


def look_up(table, index, count, splits):
    hot = one_hot_rows(256, index & 255)
    found = dot_nn(table, jnp.concatenate([hot] * splits, axis=0))
    return pick_rows(found, index >> 8, count)


def route(lists_ref, counts_ref, send_ref, slot_ref, pos_ref, upper):
    upper[...] = jnp.where(iota((256, 256), 0) < iota((256, 256), 1), 1.0, 0.0).astype(BF16)
    holder_id = iota((N_DEV, 256), 0)
    lane = iota((1, 256), 1)
    rank_id = iota((N_DEV, 256), 0) & 63
    group = 4

    def tiles(i, state):
        carry, sums = state
        hots, ranks = [], []
        ones = []
        flats = [lists_ref[pl.ds(i * group + u, 1), :] for u in range(group)]
        lives = [lane < counts_ref[i * group + u] for u in range(group)]
        holders = [jnp.where(lives[u], flats[u] // SURF, -1) for u in range(group)]
        ones = [jnp.where(holder_id == h, 1.0, 0.0) for h in holders]
        counts = dot_nn(jnp.concatenate(ones, axis=0).astype(BF16), upper[...])
        left, right = [], []
        for u in range(group):
            count = counts[u * N_DEV : u * N_DEV + N_DEV] + carry
            rank = jnp.sum(ones[u] * count, axis=0, keepdims=True).astype(I32)
            carry = carry + jnp.sum(ones[u], axis=1, keepdims=True)
            pos_ref[pl.ds(i * group + u, 1), :] = jnp.where(
                lives[u], holders[u] * SHARE + rank, -1
            )
            local = flats[u] % SURF
            values = [
                (local // 64).astype(F32),
                (local % 64).astype(F32),
                lane.astype(F32),
                jnp.full((1, 256), i * group + u, I32).astype(F32),
            ]
            left.append(jnp.concatenate([ones[u] * v for v in values], axis=0).astype(BF16))
            right.append(jnp.where(rank_id == rank, 1.0, 0.0).astype(BF16))
        sums = sums + dot_nt(jnp.concatenate(left, axis=1), jnp.concatenate(right, axis=1))
        return carry, sums

    _, sums = lax.fori_loop(
        0, TILES // group, tiles, (jnp.zeros((N_DEV, 1), F32), jnp.zeros((4 * N_DEV, 128), F32))
    )
    named = (iota((N_DEV, 128), 1) & 63) < SHARE
    local = (sums[0:128] * 64.0 + sums[128:256]).astype(I32)
    slot = (sums[384:512] * 256.0 + sums[256:384]).astype(I32)
    send_ref[:, 0, :] = jnp.where(named, local, -1)
    slot_ref[:, 0, :] = jnp.where(named, slot, -1)


def build_rows(splat_ref, position_ref, harmonics_ref, cams_ref, table):
    cams = cams_ref[...]

    def build(h, c):
        lanes = pl.ds(pl.multiple_of(h * 256, 256), 256)
        (x, y, z), _ = directions([position_ref[d : d + 1, lanes] for d in range(3)], cams)
        basis = sh_basis(x, y, z)
        colors = []
        for ch in range(3):
            total = jnp.zeros_like(x)
            for b in range(16):
                total = total + harmonics_ref[ch * 16 + b : ch * 16 + b + 1, lanes] * basis[b]
            colors.append(jnp.maximum(total + 0.5, 0.0))
        splat = splat_ref[:, lanes]
        for v in range(4):
            rows = jnp.concatenate(
                [splat] + [col[v : v + 1] for col in colors] + [jnp.zeros((2, 256), F32)], axis=0
            )
            table[v, pl.ds(pl.multiple_of(h * 16, 16), 16), :] = jnp.concatenate(split3(rows), axis=1)
        return c

    lax.fori_loop(0, 16, build, 0)


def fetch_rows(step, got_ref, out_ref, table):
    index = index_blocks(got_ref, step * 16) + index_blocks(got_ref, step * 16 + 8)
    found = halves([look_up(table[step // 2], i, 16, 3) for i in wide(index)])
    write_messages(out_ref, step * 16, found[0:3])
    write_messages(out_ref, step * 16 + 8, found[3:6])


def monomials(pixel, which):
    px = ((pixel & 15).astype(F32) - 7.5) * 0.125
    py = ((pixel >> 4).astype(F32) - 7.5) * 0.125
    m = jnp.where(which == 0, 1.0, 0.0)
    for n, value in ((1, px), (2, py), (3, px * px), (4, px * py), (5, py * py)):
        m = jnp.where(which == n, value, m)
    return m


def stack(parts):
    return jnp.concatenate(parts, axis=0)


def beside(parts):
    return jnp.concatenate(parts, axis=1)


def unstack(x, rows, count):
    return [x[rows * i : rows * i + rows] for i in range(count)]


def arrange_rows(recv_ref, table):
    def unpack(step, c):
        blocks = message_blocks(recv_ref, step * 16) + message_blocks(recv_ref, step * 16 + 8)
        for n, g in enumerate(wide(blocks)):
            table[pl.ds(pl.multiple_of(step * 48 + n * 16, 16), 16), :] = beside(split2(g))
        return c

    lax.fori_loop(0, 8, unpack, 0)


def composite(
    pos_ref, counts_ref, color_ref, normal_ref, loss_ref, table, grads, before, sign, after, mono_col
):
    j, k = iota((512, 256), 0) & 255, iota((512, 256), 1)
    before[...] = jnp.where(j < k, 1.0, 0.0).astype(BF16)
    sign[...] = jnp.where(j < k, 1.0, jnp.where(j > k, -1.0, 0.0)).astype(BF16)
    after[...] = jnp.where(j > k, 1.0, 0.0).astype(BF16)
    col = iota((256, 128), 1)
    mono_col[...] = jnp.where(col < 24, monomials(iota((256, 128), 0), col & 7), 0.0).astype(BF16)

    lane = iota((1, 256), 1)
    row8 = iota((8, 256), 0)
    y_scale = jnp.where(row8 < 3, -0.25, jnp.where(row8 < 6, 1.0, 0.0))
    y_const = jnp.where(row8 == 6, 0.25, 0.0)
    kappa = 2.0 / 256.0
    dv_scale = jnp.where(row8 < 3, -0.25 * kappa, jnp.where(row8 < 6, kappa, 0.0))
    px_low = (row8.astype(F32) - 7.5) * 0.125
    px_high = px_low + 1.0
    zero1 = jnp.zeros((1, 256), F32)
    zero8 = jnp.zeros((8, 256), F32)

    def tiles(i, c):
        ts = [i * GROUP + u for u in range(GROUP)]
        each = range(GROUP)
        rows = []
        for t in ts:
            rows.append(look_up(table[...], pos_ref[pl.ds(t, 1), :], 24, 2))
        coefs, sigs = [], []
        for u, t in enumerate(ts):
            a0, a1, a2, b0, b1, b2, logit = [rows[u][r : r + 1] for r in range(7)]
            s = -0.5 * LOG2E
            grow = jnp.exp(-logit)
            offset = jnp.log(1.0 + grow) * (-LOG2E) + LOG2_TOP
            sigs.append(1.0 / (1.0 + grow))
            c0 = jnp.where(lane < counts_ref[t], s * (a0 * a0 + b0 * b0) + offset, -1e4)
            coef = stack(
                [
                    c0,
                    (2.0 * s) * (a0 * a1 + b0 * b1),
                    (2.0 * s) * (a0 * a2 + b0 * b2),
                    s * (a1 * a1 + b1 * b1),
                    (2.0 * s) * (a1 * a2 + b1 * b2),
                    s * (a2 * a2 + b2 * b2),
                    zero1,
                    zero1,
                ]
            )
            coefs.append(stack([p.astype(F32) for p in split3(coef)] + [zero8]).astype(BF16))
        depth = [rows[u][7:8] for u in each]
        v8 = [rows[u][8:16] for u in each]
        alpha = [jnp.exp2(dot_nn(mono_col[:, 0:32], coefs[u])) for u in each]
        logkeep = [jnp.log(1.0 - alpha[u]) for u in each]
        seen = unstack(
            dot_nn(stack([beside(split2(logkeep[u])) for u in each]), before[...]), 256, GROUP
        )
        w = [alpha[u] * jnp.exp(seen[u]) for u in each]
        w2 = [beside(split2(w[u])) for u in each]
        sums = unstack(
            dot_nn(stack(w2 + [beside(split2(w[u] * depth[u])) for u in each]), sign[...]),
            256,
            2 * GROUP,
        )
        am, bm = sums[0:GROUP], sums[GROUP:]
        resid, x32, y = [], [], []
        for u, t in enumerate(ts):
            v16 = stack([p.astype(F32) for p in split2(v8[u])]).astype(BF16)
            shown = dot_nt(beside([v16, v16]), w2[u])
            shown = shown[0:8] + shown[8:16]
            resid.append(shown[3:6] - color_ref[:, t, :])
        for u, t in enumerate(ts):
            x8 = stack([normal_ref[:, t, :], resid[u], zero1 + 1.0, zero1])
            xh, xl = [p.astype(F32) for p in split2(x8)]
            yh, yl = [p.astype(F32) for p in split2(v8[u] * y_scale + y_const)]
            x32.append(stack([xh, xl, xh, zero8]).astype(BF16))
            y32 = stack([yh, yh, yl, zero8]).astype(BF16)
            y.append((dot_tn(x32[u], y32) + (depth[u] * am[u] - bm[u])) * w[u])
        behind = unstack(
            dot_nn(stack([beside(split2(y[u])) for u in each]), after[...]), 256, GROUP
        )
        for u, t in enumerate(ts):
            hgrad = y[u] - behind[u] * (alpha[u] * jnp.exp(-logkeep[u]))
            low = [zero8] * 3
            high = [zero8] * 3
            for r in range(16):
                low[0] = low[0] + hgrad[r * 16 : r * 16 + 8]
                high[0] = high[0] + hgrad[r * 16 + 8 : r * 16 + 16]
                for n in (1, 2):
                    low[n] = low[n] + low[n - 1]
                    high[n] = high[n] + high[n - 1]

            def moment(first, second):
                return jnp.sum(first + second, axis=0, keepdims=True) * (-kappa)

            def rows_of(f):
                return f[0], 1.0625 * f[0] - 0.125 * f[1], (
                    1.12890625 * f[0] - 0.28125 * f[1] + 0.03125 * f[2]
                )

            low, high = rows_of(low), rows_of(high)
            m0 = moment(low[0], high[0])
            m1 = moment(low[0] * px_low, high[0] * px_high)
            m2 = moment(low[1], high[1])
            m3 = moment(low[0] * (px_low * px_low), high[0] * (px_high * px_high))
            m4 = moment(low[1] * px_low, high[1] * px_high)
            m5 = moment(low[2], high[2])
            x16 = x32[u][0:16]
            dv = dot_nn(beside([x16, x16]), stack([w2[u][:, 0:256], w2[u][:, 256:512]]))
            dv = dv[0:8] + dv[8:16]
            ga = jnp.sum(w[u] * am[u], axis=0, keepdims=True)
            a0, a1, a2, b0, b1, b2 = [rows[u][r : r + 1] for r in range(6)]
            out = stack(
                [
                    a0 * m0 + a1 * m1 + a2 * m2,
                    a0 * m1 + a1 * m3 + a2 * m4,
                    a0 * m2 + a1 * m4 + a2 * m5,
                    b0 * m0 + b1 * m1 + b2 * m2,
                    b0 * m1 + b1 * m3 + b2 * m4,
                    b0 * m2 + b1 * m4 + b2 * m5,
                    (sigs[u] - 1.0) * m0,
                    kappa * ga,
                    dv * dv_scale,
                ]
            )
            grads[pl.ds(pl.multiple_of(t * 16, 16), 16), :] = beside(split2(out))
            facing = v8[u][0:3] * dv[0:3]
            loss = (
                jnp.sum(resid[u] * resid[u] - 0.5 * facing, axis=0, keepdims=True)
                + 2.0 * (depth[u] * ga)
                + 0.5 * dv[6:7]
            ) * (1.0 / 256.0)
            loss_ref[pl.ds(t, 1), :] = loss[:, 0:128] + loss[:, 128:256]
        return c

    lax.fori_loop(0, TILES // GROUP, tiles, 0)


def return_rows(step, slot_ref, out_ref, grads):
    index = index_blocks(slot_ref, step * 16) + index_blocks(slot_ref, step * 16 + 8)
    found = halves([look_up(grads[...], i, 32, 2) for i in wide(index)])
    write_messages(out_ref, step * 16, found[0:3])
    write_messages(out_ref, step * 16 + 8, found[3:6])


def sum_rows(step, back_ref, got_ref, acc):
    index = wide(index_blocks(got_ref, step * 16) + index_blocks(got_ref, step * 16 + 8))
    data = wide(message_blocks(back_ref, step * 16) + message_blocks(back_ref, step * 16 + 8))
    left, right = [], []
    for i, d in zip(index, data):
        hot = one_hot_rows(256, i & 255)
        both = beside([p.astype(F32) for p in split2(d)])
        high = beside([i >> 8, i >> 8])
        left.append(stack([jnp.where(high == h, both, 0.0).astype(BF16) for h in range(16)]))
        right += [hot, hot]
    acc[step // 2] += dot_nt(beside(left), beside(right))


def finish_grads(position_ref, harmonics_ref, cams_ref, gs_ref, gp_ref, gh_ref, acc):
    cams = cams_ref[...]

    def finish(h, c):
        lanes = pl.ds(pl.multiple_of(h * 256, 256), 256)
        views = [acc[v, pl.ds(pl.multiple_of(h * 16, 16), 16), :] for v in range(4)]
        total = (views[0] + views[1]) + (views[2] + views[3])
        gs_ref[:, lanes] = total[0:11]
        dirs, length = directions([position_ref[d : d + 1, lanes] for d in range(3)], cams)
        x, y, z = dirs
        basis = sh_basis(x, y, z)
        dbasis = [jnp.zeros_like(x) for _ in range(16)]
        for ch in range(3):
            coeffs = [harmonics_ref[ch * 16 + b : ch * 16 + b + 1, lanes] for b in range(16)]
            value = jnp.zeros_like(x)
            for b in range(16):
                value = value + coeffs[b] * basis[b]
            value = value + 0.5
            dcol = stack([views[v][11 + ch : 12 + ch] for v in range(4)])
            dcol = dcol * jnp.where(value > 0.0, 1.0, jnp.where(value == 0.0, 0.5, 0.0))
            for b in range(16):
                gh_ref[ch * 16 + b : ch * 16 + b + 1, lanes] = jnp.sum(
                    dcol * basis[b], axis=0, keepdims=True
                )
                dbasis[b] = dbasis[b] + dcol * coeffs[b]
        grads = sh_basis_back(x, y, z, dbasis)
        along = grads[0] * x + grads[1] * y + grads[2] * z
        for d in range(3):
            gp_ref[d : d + 1, lanes] = jnp.sum(
                (grads[d] - dirs[d] * along) / length, axis=0, keepdims=True
            )
        return c

    lax.fori_loop(0, 16, finish, 0)


def greet_all(me):
    barrier = pltpu.get_barrier_semaphore()

    def greet(i, c):
        pl.semaphore_signal(
            barrier, inc=1, device_id=(lax.rem(me + i, N_DEV),), device_id_type=MESH
        )
        return c

    lax.fori_loop(1, N_DEV, greet, 0)


def send_block(src_ref, dst_ref, me, peer, send_sem, recv_sem):
    pltpu.make_async_remote_copy(
        src_ref=src_ref.at[peer],
        dst_ref=dst_ref.at[me],
        send_sem=send_sem,
        recv_sem=recv_sem,
        device_id=(peer,),
        device_id_type=MESH,
    ).start()


def wait_all(src_ref, dst_ref, me, send_sem, recv_sem):
    pltpu.make_async_remote_copy(
        src_ref=src_ref.at[pl.ds(0, N_DEV - 1)],
        dst_ref=dst_ref.at[pl.ds(0, N_DEV - 1)],
        send_sem=send_sem,
        recv_sem=recv_sem,
        device_id=(me,),
        device_id_type=MESH,
    ).wait()


def make_and_send(make, src_ref, dst_ref, me, send_sem, recv_sem):
    def steps(i, c):
        step = lax.rem(me // 16 + i, 8)
        make(step)

        def send(s, d):
            peer = step * 16 + s

            @pl.when(peer != me)
            def _():
                send_block(src_ref, dst_ref, me, peer, send_sem, recv_sem)

            return d

        lax.fori_loop(0, 16, send, 0)
        return c

    lax.fori_loop(0, 8, steps, 0)
    dst_ref[me] = src_ref[me]
    wait_all(src_ref, dst_ref, me, send_sem, recv_sem)


def step_kernel(
    splat_ref, position_ref, harmonics_ref, cams_ref, lists_ref, counts_ref, color_ref, normal_ref,
    gs_ref, gp_ref, gh_ref, loss_ref,
    ask, got, slot, pos, rows, recv, grad_rows, back, upper, surfels, table, grads, acc,
    before, sign, after, mono_col, send_sem, recv_sem,
):
    me = lax.axis_index("surf")
    greet_all(me)
    route(lists_ref, counts_ref, ask, slot, pos, upper)
    pl.semaphore_wait(pltpu.get_barrier_semaphore(), N_DEV - 1)

    def request(i, c):
        send_block(ask, got, me, lax.rem(me + i, N_DEV), send_sem.at[0], recv_sem.at[0])
        return c

    lax.fori_loop(1, N_DEV, request, 0)
    got[me] = ask[me]
    build_rows(splat_ref, position_ref, harmonics_ref, cams_ref, surfels)
    wait_all(ask, got, me, send_sem.at[0], recv_sem.at[0])
    make_and_send(
        lambda step: fetch_rows(step, got, rows, surfels),
        rows, recv, me, send_sem.at[1], recv_sem.at[1],
    )
    arrange_rows(recv, table)
    composite(
        pos, counts_ref, color_ref, normal_ref, loss_ref, table, grads, before, sign, after, mono_col
    )
    make_and_send(
        lambda step: return_rows(step, slot, grad_rows, grads),
        grad_rows, back, me, send_sem.at[2], recv_sem.at[2],
    )
    acc[...] = jnp.zeros_like(acc)

    def add(step, c):
        sum_rows(step, back, got, acc)
        return c

    lax.fori_loop(0, 8, add, 0)
    finish_grads(position_ref, harmonics_ref, cams_ref, gs_ref, gp_ref, gh_ref, acc)


VM = pl.BlockSpec(memory_space=pltpu.VMEM)
SM = pl.BlockSpec(memory_space=pltpu.SMEM)
LIMIT = 48 * 1024 * 1024


def on_device(
    splat, position, harmonics, cameras, tile_lists, tile_counts, target_color, target_normal
):
    gs, gp, gh, loss = pl.pallas_call(
        step_kernel,
        out_shape=(
            jax.ShapeDtypeStruct((11, SURF), F32),
            jax.ShapeDtypeStruct((3, SURF), F32),
            jax.ShapeDtypeStruct((48, SURF), F32),
            jax.ShapeDtypeStruct((TILES, 128), F32),
        ),
        in_specs=[VM, VM, VM, VM, VM, SM, VM, VM],
        out_specs=(VM, VM, VM, VM),
        scratch_shapes=[
            pltpu.VMEM((N_DEV, 1, 128), I32),
            pltpu.VMEM((N_DEV, 1, 128), I32),
            pltpu.VMEM((N_DEV, 1, 128), I32),
            pltpu.VMEM((TILES, 256), I32),
            pltpu.VMEM((N_DEV, 8, 128), F32),
            pltpu.VMEM((N_DEV, 8, 128), F32),
            pltpu.VMEM((N_DEV, 8, 128), F32),
            pltpu.VMEM((N_DEV, 8, 128), F32),
            pltpu.VMEM((256, 256), BF16),
            pltpu.VMEM((4, 256, 768), BF16),
            pltpu.VMEM((384, 512), BF16),
            pltpu.VMEM((512, 512), BF16),
            pltpu.VMEM((4, 256, 256), F32),
            pltpu.VMEM((512, 256), BF16),
            pltpu.VMEM((512, 256), BF16),
            pltpu.VMEM((512, 256), BF16),
            pltpu.VMEM((256, 128), BF16),
            pltpu.SemaphoreType.DMA((3,)),
            pltpu.SemaphoreType.DMA((3,)),
        ],
        compiler_params=pltpu.CompilerParams(
            collective_id=0, has_side_effects=True, vmem_limit_bytes=LIMIT
        ),
        name="surfel_step",
    )(splat, position, harmonics, cameras, tile_lists, tile_counts, target_color, target_normal)
    return gs, gp, gh, jnp.sum(loss, axis=1)


def solution(mesh):
    return jax.shard_map(
        on_device,
        mesh=mesh,
        in_specs=(
            P(None, "surf"),
            P(None, "surf"),
            P(None, "surf"),
            P(),
            P("surf", None),
            P("surf"),
            P(None, "surf", None),
            P(None, "surf", None),
        ),
        out_specs=(P(None, "surf"), P(None, "surf"), P(None, "surf"), P("surf")),
        check_vma=False,
    )
```

time: 172 us -> 90.6 us (0.53)
  Pallas kernels: 161 us -> 79.9 us
    pallas_call x7 -> x1, Pallas kernels: 161 us -> 79.9 us  [on_device(): pl.pallas_call(step_kernel, out_shape=(jax.ShapeDtypeStruct((11, SURF), F...]
    unnamed x34 -> x19, local copies, waits for them, and re-layouts: 8.64 us -> 9 us
where the time goes in v2:
time: 90.6 us; the launch traced here: 90.2 us
  Pallas kernels  79.9 us (88%)
  local copies, waits for them, and re-layouts  9 us (10%)
    pallas_call x1, Pallas kernels, on_device(): pl.pallas_call(step_kernel, out_shape=(jax.ShapeDtypeStruct((11, SURF), F...  79.9 us
    unnamed x19, local copies, waits for them, and re-layouts  9 us

profile of v2, /device:TPU:1, one launch (start us, length us, event | category | flops | bytes accessed | tf_op | source)
XLA Modules:
  0.0 90.2 jit_solution(1659994681213281827)
XLA Ops:
  0.6 0.0 copy-start
  0.6 1.1 %copy-done = f32[48,4096]{1,0:T(8,128)S(1)} copy-done((f32[48,4096]{1,0:T(8,128)S(1)}, f32[48,4096]{1,0:T(8,128)}, u32[]{:S(2)}) %copy-start) | copy-done | bytes 786456
  1.8 0.0 copy-start.1
  1.8 0.9 %copy-done.1 = f32[11,4096]{1,0:T(8,128)S(1)} copy-done((f32[11,4096]{1,0:T(8,128)S(1)}, f32[11,4096]{1,0:T(8,128)}, u32[]{:S(2)}) %copy-start.1) | copy-done | bytes 180248
  2.7 0.0 copy-start.2
  2.7 0.9 copy-done.2
  3.6 0.0 copy-start.3
  3.6 0.9 copy-done.3
  4.5 0.0 copy-start.4
  4.5 0.8 copy-done.4
  5.3 0.0 copy-start.5
  5.3 0.8 copy-done.5
  6.1 0.0 copy-start.6
  6.1 0.7 copy-done.6
  6.8 0.0 copy-start.7
  6.8 0.7 copy-done.7
  7.4 79.9 %surfel_step.1 = (f32[11,4096]{1,0:T(8,128)S(1)}, f32[3,4096]{1,0:T(4,128)S(1)}, f32[48,4096]{1,0:T(8,128)S(1)}, f32[32,128]{1,0:T(8,128)S(1)}) custom-call(f32[11,4096]{1,0:T(8,128)S(1)} %copy-done.1, f32[3,4096]{1,0:T(4,128)S(1)} %copy-done.4, f32[48,4096]{1,0:T(8,128)S(1)} %copy-done, f32[4,3]{1,0:T(4,128)S(1)} %copy-done.6, s32[32,256]{1,0:T(8,128)S(1)} %copy-done.5, ...), custom_call_target="tpu_custom_call" | custom-call | tf_op jit(solution)/shard_map/surfel_step/pallas_call | solution.py:611
  87.4 0.6 reduce_sum.9
  88.0 0.7 copy.15
  88.7 0.6 copy.16
  89.4 0.9 copy.17
Async XLA Ops:
  0.6 1.1 %copy-start = (f32[48,4096]{1,0:T(8,128)S(1)}, f32[48,4096]{1,0:T(8,128)}, u32[]{:S(2)}) copy-start(f32[48,4096]{1,0:T(8,128)} %harmonics_ref.1) | copy-start | bytes 2359300
  1.8 0.9 %copy-start.1 = (f32[11,4096]{1,0:T(8,128)S(1)}, f32[11,4096]{1,0:T(8,128)}, u32[]{:S(2)}) copy-start(f32[11,4096]{1,0:T(8,128)} %splat_ref.1) | copy-start | bytes 540676
  2.7 0.9 copy-start.2
  3.6 0.9 copy-start.3
  4.5 0.8 copy-start.4
  5.3 0.8 copy-start.5
  6.1 0.7 copy-start.6
  6.8 0.7 copy-start.7

commit v3 on v2

--- a/solution.py
+++ b/solution.py
@@ -17,7 +17,7 @@
 SHARE = 48
 LOG2E = 1.4426950408889634
 LOG2_TOP = -0.07400058144377693
-GROUP = 4
+GROUP = 8
 
 sh_zero = 0.28209479177387814
 sh_one = 0.4886025119029199
@@ -203,8 +203,13 @@
     return pick_rows(found, index >> 8, count)
 
 
-def route(lists_ref, counts_ref, send_ref, slot_ref, pos_ref, upper):
-    upper[...] = jnp.where(iota((256, 256), 0) < iota((256, 256), 1), 1.0, 0.0).astype(BF16)
+def tall(row):
+    return jnp.concatenate([jnp.broadcast_to(row, (16, 256)).astype(BF16)] * (N_DEV // 16), axis=0)
+
+
+def route(lists_ref, counts_ref, send_ref, slot_ref, pos_ref, upper, greet):
+    col = iota((256, 384), 1)
+    upper[...] = jnp.where((iota((256, 384), 0) < col) | (col > 255), 1.0, 0.0).astype(BF16)
     holder_id = iota((N_DEV, 256), 0)
     lane = iota((1, 256), 1)
     rank_id = iota((N_DEV, 256), 0) & 63
@@ -212,72 +217,111 @@
 
     def tiles(i, state):
         carry, sums = state
-        hots, ranks = [], []
-        ones = []
+        greet(i)
         flats = [lists_ref[pl.ds(i * group + u, 1), :] for u in range(group)]
         lives = [lane < counts_ref[i * group + u] for u in range(group)]
         holders = [jnp.where(lives[u], flats[u] // SURF, -1) for u in range(group)]
         ones = [jnp.where(holder_id == h, 1.0, 0.0) for h in holders]
-        counts = dot_nn(jnp.concatenate(ones, axis=0).astype(BF16), upper[...])
+        marks = [o.astype(BF16) for o in ones]
+        counts = dot_nn(jnp.concatenate(marks, axis=0), upper[...])
         left, right = [], []
         for u in range(group):
-            count = counts[u * N_DEV : u * N_DEV + N_DEV] + carry
-            rank = jnp.sum(ones[u] * count, axis=0, keepdims=True).astype(I32)
-            carry = carry + jnp.sum(ones[u], axis=1, keepdims=True)
+            count = counts[u * N_DEV : u * N_DEV + N_DEV]
+            rank = jnp.sum(
+                ones[u] * (count[:, 0:256] + beside([carry, carry])), axis=0, keepdims=True
+            ).astype(I32)
+            carry = carry + count[:, 256:384]
             pos_ref[pl.ds(i * group + u, 1), :] = jnp.where(
                 lives[u], holders[u] * SHARE + rank, -1
             )
             local = flats[u] % SURF
             values = [
-                (local // 64).astype(F32),
-                (local % 64).astype(F32),
+                (local // 8 - 256).astype(F32),
+                (local % 8 * TILES + (i * group + u)).astype(F32),
                 lane.astype(F32),
-                jnp.full((1, 256), i * group + u, I32).astype(F32),
             ]
-            left.append(jnp.concatenate([ones[u] * v for v in values], axis=0).astype(BF16))
+            left.append(jnp.concatenate([marks[u] * tall(v) for v in values], axis=0))
             right.append(jnp.where(rank_id == rank, 1.0, 0.0).astype(BF16))
         sums = sums + dot_nt(jnp.concatenate(left, axis=1), jnp.concatenate(right, axis=1))
         return carry, sums
 
     _, sums = lax.fori_loop(
-        0, TILES // group, tiles, (jnp.zeros((N_DEV, 1), F32), jnp.zeros((4 * N_DEV, 128), F32))
+        0, TILES // group, tiles, (jnp.zeros((N_DEV, 128), F32), jnp.zeros((3 * N_DEV, 128), F32))
     )
     named = (iota((N_DEV, 128), 1) & 63) < SHARE
-    local = (sums[0:128] * 64.0 + sums[128:256]).astype(I32)
-    slot = (sums[384:512] * 256.0 + sums[256:384]).astype(I32)
+    low = sums[128:256].astype(I32)
+    local = (sums[0:128].astype(I32) + 256) * 8 + low // TILES
+    slot = low % TILES * 256 + sums[256:384].astype(I32)
     send_ref[:, 0, :] = jnp.where(named, local, -1)
     slot_ref[:, 0, :] = jnp.where(named, slot, -1)
 
 
-def build_rows(splat_ref, position_ref, harmonics_ref, cams_ref, table):
+def put_row(tmp, b, value):
+    for half in range(2):
+        tmp[half * 128 + b * 8 : half * 128 + b * 8 + 4, :] = value[:, half * 128 : half * 128 + 128]
+
+
+def row_of(tmp, b):
+    return jnp.concatenate(
+        [tmp[half * 128 + b * 8 : half * 128 + b * 8 + 4, :] for half in range(2)], axis=1
+    )
+
+
+def column(tmp, v):
+    return jnp.concatenate(
+        [tmp[pl.ds(half * 128 + v, 16, stride=8), :] for half in range(2)], axis=1
+    )
+
+
+def build_rows(
+    splat_ref, position_ref, harmonics_ref, cams_ref, table, basis_ref, dirs_ref, mask_ref, tmp, request
+):
     cams = cams_ref[...]
 
-    def build(h, c):
+    def build(h, own):
+        request(h, own)
         lanes = pl.ds(pl.multiple_of(h * 256, 256), 256)
-        (x, y, z), _ = directions([position_ref[d : d + 1, lanes] for d in range(3)], cams)
-        basis = sh_basis(x, y, z)
-        colors = []
-        for ch in range(3):
-            total = jnp.zeros_like(x)
-            for b in range(16):
-                total = total + harmonics_ref[ch * 16 + b : ch * 16 + b + 1, lanes] * basis[b]
-            colors.append(jnp.maximum(total + 0.5, 0.0))
+        dirs, length = directions([position_ref[d : d + 1, lanes] for d in range(3)], cams)
+        for d, value in enumerate(dirs + [1.0 / length]):
+            dirs_ref[d, :, lanes] = value
+        for b, value in enumerate(sh_basis(*dirs)):
+            put_row(tmp, b, value)
         splat = splat_ref[:, lanes]
+        coeffs = [harmonics_ref[ch * 16 : ch * 16 + 16, lanes] for ch in range(3)]
         for v in range(4):
-            rows = jnp.concatenate(
-                [splat] + [col[v : v + 1] for col in colors] + [jnp.zeros((2, 256), F32)], axis=0
-            )
-            table[v, pl.ds(pl.multiple_of(h * 16, 16), 16), :] = jnp.concatenate(split3(rows), axis=1)
-        return c
-
-    lax.fori_loop(0, 16, build, 0)
-
-
-def fetch_rows(step, got_ref, out_ref, table):
-    index = index_blocks(got_ref, step * 16) + index_blocks(got_ref, step * 16 + 8)
-    found = halves([look_up(table[step // 2], i, 16, 3) for i in wide(index)])
-    write_messages(out_ref, step * 16, found[0:3])
-    write_messages(out_ref, step * 16 + 8, found[3:6])
+            basis = column(tmp, v)
+            basis_ref[v, :, lanes] = basis
+            colors = []
+            for ch in range(3):
+                value = jnp.sum(coeffs[ch] * basis, axis=0, keepdims=True) + 0.5
+                mask_ref[ch * 4 + v : ch * 4 + v + 1, lanes] = jnp.where(
+                    value > 0.0, 1.0, jnp.where(value == 0.0, 0.5, 0.0)
+                )
+                colors.append(jnp.maximum(value, 0.0))
+            rows = jnp.concatenate([splat] + colors + [jnp.zeros((2, 256), F32)], axis=0)
+            table[v, pl.ds(pl.multiple_of(h * 16, 16), 16), :] = jnp.concatenate(split2(rows), axis=1)
+
+    for i in range(4):
+        lax.fori_loop(4 * i, 4 * i + 4, lambda h, c: build(h, i) or c, 0)
+
+
+def plane_blocks(blocks_of_eight, ref, plane):
+    return wide([b for s in range(4) for b in blocks_of_eight(ref, plane * 32 + s * 8)])
+
+
+def write_plane(ref, plane, index, count, table, between):
+    chunks = []
+    for n, i in enumerate(index):
+        chunks.append(look_up(table, i, count, 2))
+        between(n)
+    blocks = halves(chunks)
+    for s in range(4):
+        write_messages(ref, plane * 32 + s * 8, blocks[3 * s : 3 * s + 3])
+
+
+def fetch_rows(plane, got_ref, out_ref, table, between):
+    index = plane_blocks(index_blocks, got_ref, plane)
+    write_plane(out_ref, plane, index, 16, table[plane], between)
 
 
 def monomials(pixel, which):
@@ -301,19 +345,12 @@
     return [x[rows * i : rows * i + rows] for i in range(count)]
 
 
-def arrange_rows(recv_ref, table):
-    def unpack(step, c):
-        blocks = message_blocks(recv_ref, step * 16) + message_blocks(recv_ref, step * 16 + 8)
-        for n, g in enumerate(wide(blocks)):
-            table[pl.ds(pl.multiple_of(step * 48 + n * 16, 16), 16), :] = beside(split2(g))
-        return c
-
-    lax.fori_loop(0, 8, unpack, 0)
-
-
-def composite(
-    pos_ref, counts_ref, color_ref, normal_ref, loss_ref, table, grads, before, sign, after, mono_col
-):
+def arrange_rows(plane, recv_ref, table):
+    for n, g in enumerate(plane_blocks(message_blocks, recv_ref, plane)):
+        table[pl.ds(pl.multiple_of(plane * 96 + n * 16, 16), 16), :] = beside(split2(g))
+
+
+def constants(before, sign, after, mono_col):
     j, k = iota((512, 256), 0) & 255, iota((512, 256), 1)
     before[...] = jnp.where(j < k, 1.0, 0.0).astype(BF16)
     sign[...] = jnp.where(j < k, 1.0, jnp.where(j > k, -1.0, 0.0)).astype(BF16)
@@ -321,6 +358,10 @@
     col = iota((256, 128), 1)
     mono_col[...] = jnp.where(col < 24, monomials(iota((256, 128), 0), col & 7), 0.0).astype(BF16)
 
+
+def composite(
+    pos_ref, counts_ref, color_ref, normal_ref, loss_ref, table, grads, before, sign, after, mono_col
+):
     lane = iota((1, 256), 1)
     row8 = iota((8, 256), 0)
     y_scale = jnp.where(row8 < 3, -0.25, jnp.where(row8 < 6, 1.0, 0.0))
@@ -447,56 +488,50 @@
     lax.fori_loop(0, TILES // GROUP, tiles, 0)
 
 
-def return_rows(step, slot_ref, out_ref, grads):
-    index = index_blocks(slot_ref, step * 16) + index_blocks(slot_ref, step * 16 + 8)
-    found = halves([look_up(grads[...], i, 32, 2) for i in wide(index)])
-    write_messages(out_ref, step * 16, found[0:3])
-    write_messages(out_ref, step * 16 + 8, found[3:6])
-
-
-def sum_rows(step, back_ref, got_ref, acc):
-    index = wide(index_blocks(got_ref, step * 16) + index_blocks(got_ref, step * 16 + 8))
-    data = wide(message_blocks(back_ref, step * 16) + message_blocks(back_ref, step * 16 + 8))
+def return_rows(plane, slot_ref, out_ref, grads, between):
+    index = plane_blocks(index_blocks, slot_ref, plane)
+    write_plane(out_ref, plane, index, 32, grads[...], between)
+
+
+def sum_rows(plane, back_ref, got_ref, acc, between):
+    index = plane_blocks(index_blocks, got_ref, plane)
+    data = plane_blocks(message_blocks, back_ref, plane)
     left, right = [], []
-    for i, d in zip(index, data):
+    for n, (i, d) in enumerate(zip(index, data)):
+        between(n)
         hot = one_hot_rows(256, i & 255)
         both = beside([p.astype(F32) for p in split2(d)])
         high = beside([i >> 8, i >> 8])
         left.append(stack([jnp.where(high == h, both, 0.0).astype(BF16) for h in range(16)]))
         right += [hot, hot]
-    acc[step // 2] += dot_nt(beside(left), beside(right))
-
-
-def finish_grads(position_ref, harmonics_ref, cams_ref, gs_ref, gp_ref, gh_ref, acc):
-    cams = cams_ref[...]
-
+    acc[plane] = dot_nt(beside(left), beside(right))
+
+
+def finish_grads(harmonics_ref, basis_ref, dirs_ref, mask_ref, tmp, gs_ref, gp_ref, gh_ref, acc):
     def finish(h, c):
         lanes = pl.ds(pl.multiple_of(h * 256, 256), 256)
         views = [acc[v, pl.ds(pl.multiple_of(h * 16, 16), 16), :] for v in range(4)]
         total = (views[0] + views[1]) + (views[2] + views[3])
         gs_ref[:, lanes] = total[0:11]
-        dirs, length = directions([position_ref[d : d + 1, lanes] for d in range(3)], cams)
-        x, y, z = dirs
-        basis = sh_basis(x, y, z)
-        dbasis = [jnp.zeros_like(x) for _ in range(16)]
+        dcol = [
+            [views[v][11 + ch : 12 + ch] * mask_ref[ch * 4 + v : ch * 4 + v + 1, lanes] for v in range(4)]
+            for ch in range(3)
+        ]
+        basis = [basis_ref[v, :, lanes] for v in range(4)]
+        coeffs = [harmonics_ref[ch * 16 : ch * 16 + 16, lanes] for ch in range(3)]
         for ch in range(3):
-            coeffs = [harmonics_ref[ch * 16 + b : ch * 16 + b + 1, lanes] for b in range(16)]
-            value = jnp.zeros_like(x)
-            for b in range(16):
-                value = value + coeffs[b] * basis[b]
-            value = value + 0.5
-            dcol = stack([views[v][11 + ch : 12 + ch] for v in range(4)])
-            dcol = dcol * jnp.where(value > 0.0, 1.0, jnp.where(value == 0.0, 0.5, 0.0))
-            for b in range(16):
-                gh_ref[ch * 16 + b : ch * 16 + b + 1, lanes] = jnp.sum(
-                    dcol * basis[b], axis=0, keepdims=True
-                )
-                dbasis[b] = dbasis[b] + dcol * coeffs[b]
-        grads = sh_basis_back(x, y, z, dbasis)
+            parts = [basis[v] * dcol[ch][v] for v in range(4)]
+            gh_ref[ch * 16 : ch * 16 + 16, lanes] = (parts[0] + parts[1]) + (parts[2] + parts[3])
+        for v in range(4):
+            dbasis = coeffs[0] * dcol[0][v] + coeffs[1] * dcol[1][v] + coeffs[2] * dcol[2][v]
+            for half in range(2):
+                tmp[pl.ds(half * 128 + v, 16, stride=8), :] = dbasis[:, half * 128 : half * 128 + 128]
+        x, y, z, inverse = [dirs_ref[d, :, lanes] for d in range(4)]
+        grads = sh_basis_back(x, y, z, [row_of(tmp, b) for b in range(16)])
         along = grads[0] * x + grads[1] * y + grads[2] * z
-        for d in range(3):
+        for d, n in enumerate((x, y, z)):
             gp_ref[d : d + 1, lanes] = jnp.sum(
-                (grads[d] - dirs[d] * along) / length, axis=0, keepdims=True
+                (grads[d] - n * along) * inverse, axis=0, keepdims=True
             )
         return c
 
@@ -507,12 +542,17 @@
     barrier = pltpu.get_barrier_semaphore()
 
     def greet(i, c):
+        for s in range(1, 16):
+            pl.semaphore_signal(
+                barrier, inc=1, device_id=(lax.rem(me + i * 15 + s, N_DEV),), device_id_type=MESH
+            )
+        return c
+
+    lax.fori_loop(0, 8, greet, 0)
+    for s in range(121, N_DEV):
         pl.semaphore_signal(
-            barrier, inc=1, device_id=(lax.rem(me + i, N_DEV),), device_id_type=MESH
+            barrier, inc=1, device_id=(lax.rem(me + s, N_DEV),), device_id_type=MESH
         )
-        return c
-
-    lax.fori_loop(1, N_DEV, greet, 0)
 
 
 def send_block(src_ref, dst_ref, me, peer, send_sem, recv_sem):
@@ -520,105 +560,181 @@
         src_ref=src_ref.at[peer],
         dst_ref=dst_ref.at[me],
         send_sem=send_sem,
-        recv_sem=recv_sem,
+        recv_sem=recv_sem.at[me // 32],
         device_id=(peer,),
         device_id_type=MESH,
     ).start()
 
 
-def wait_all(src_ref, dst_ref, me, send_sem, recv_sem):
-    pltpu.make_async_remote_copy(
-        src_ref=src_ref.at[pl.ds(0, N_DEV - 1)],
-        dst_ref=dst_ref.at[pl.ds(0, N_DEV - 1)],
+def blocks_of(ref, count, me, send_sem, recv_sem):
+    return pltpu.make_async_remote_copy(
+        src_ref=ref.at[pl.ds(0, count)],
+        dst_ref=ref.at[pl.ds(0, count)],
         send_sem=send_sem,
         recv_sem=recv_sem,
         device_id=(me,),
         device_id_type=MESH,
-    ).wait()
-
-
-def make_and_send(make, src_ref, dst_ref, me, send_sem, recv_sem):
-    def steps(i, c):
-        step = lax.rem(me // 16 + i, 8)
-        make(step)
-
-        def send(s, d):
-            peer = step * 16 + s
-
-            @pl.when(peer != me)
-            def _():
-                send_block(src_ref, dst_ref, me, peer, send_sem, recv_sem)
-
-            return d
-
-        lax.fori_loop(0, 16, send, 0)
+    )
+
+
+def plane_at(me, i, direction):
+    distance = (1, 3, 2, 0)[i]
+    return lax.rem(me // 32 + (distance if direction > 0 else (4 - distance) % 4), 4)
+
+
+def plane_sender(src_ref, dst_ref, me, i, direction, send_sem, recv_sem):
+    plane = plane_at(me, i, direction)
+
+    def send(s):
+        peer = plane * 32 + lax.rem(me % 32 + 1 + s, 32)
+        send_block(src_ref, dst_ref, me, peer, send_sem, recv_sem)
+
+    count = 31 if i == 3 else 32
+    return send, count, plane
+
+
+def between_of(sender):
+    send, count, _ = sender
+
+    def between(n):
+        for s in range(n * 6, min(n * 6 + 6, count)):
+            send(s)
+
+    return between
+
+
+def send_plane(sender):
+    send, count, _ = sender
+
+    def one(s, c):
+        send(s)
         return c
 
-    lax.fori_loop(0, 8, steps, 0)
-    dst_ref[me] = src_ref[me]
-    wait_all(src_ref, dst_ref, me, send_sem, recv_sem)
+    lax.fori_loop(0, count, one, 0)
+
+
+def nothing(n):
+    pass
+
+
+def wait_plane(ref, me, i, direction, send_sem, recv_sem):
+    plane = plane_at(me, i, direction)
+    blocks_of(ref, 32 if i < 3 else 31, me, send_sem, recv_sem.at[plane]).wait_recv()
+    return plane
 
 
 def step_kernel(
+    splat_hbm, position_hbm, harmonics_hbm, cams_hbm, lists_hbm, counts_hbm, color_hbm, normal_hbm,
+    acc, basis, dirs, mask, loss_ref,
     splat_ref, position_ref, harmonics_ref, cams_ref, lists_ref, counts_ref, color_ref, normal_ref,
-    gs_ref, gp_ref, gh_ref, loss_ref,
-    ask, got, slot, pos, rows, recv, grad_rows, back, upper, surfels, table, grads, acc,
-    before, sign, after, mono_col, send_sem, recv_sem,
+    ask, got, slot, pos, rows, recv, grad_rows, back, upper, surfels, table, grads,
+    before, sign, after, mono_col, tmp, load_sem, send_sem, ask_sem, row_sem, back_sem,
 ):
     me = lax.axis_index("surf")
+    pairs = [
+        (lists_hbm, lists_ref), (counts_hbm, counts_ref), (cams_hbm, cams_ref),
+        (position_hbm, position_ref), (harmonics_hbm, harmonics_ref), (splat_hbm, splat_ref),
+        (color_hbm, color_ref), (normal_hbm, normal_ref),
+    ]
+    loads = [
+        pltpu.make_async_copy(src, dst, load_sem.at[n]) for n, (src, dst) in enumerate(pairs)
+    ]
+    for load in loads:
+        load.start()
     greet_all(me)
-    route(lists_ref, counts_ref, ask, slot, pos, upper)
+    loads[0].wait()
+    loads[1].wait()
+    route(lists_ref, counts_ref, ask, slot, pos, upper, nothing)
     pl.semaphore_wait(pltpu.get_barrier_semaphore(), N_DEV - 1)
-
-    def request(i, c):
-        send_block(ask, got, me, lax.rem(me + i, N_DEV), send_sem.at[0], recv_sem.at[0])
-        return c
-
-    lax.fori_loop(1, N_DEV, request, 0)
     got[me] = ask[me]
-    build_rows(splat_ref, position_ref, harmonics_ref, cams_ref, surfels)
-    wait_all(ask, got, me, send_sem.at[0], recv_sem.at[0])
-    make_and_send(
-        lambda step: fetch_rows(step, got, rows, surfels),
-        rows, recv, me, send_sem.at[1], recv_sem.at[1],
-    )
-    arrange_rows(recv, table)
+    for load in loads[2:6]:
+        load.wait()
+
+    requests = [plane_sender(ask, got, me, i, 1, send_sem.at[0], ask_sem) for i in range(4)]
+
+    def request(h, i):
+        send, count, _ = requests[i]
+        for s in range(8):
+            send((h - 4 * i) * 8 + s)
+
+    def request_own(h, i):
+        send, count, _ = requests[i]
+        for s in range(7):
+            send((h - 4 * i) * 8 + s)
+
+        @pl.when(h < 15)
+        def _():
+            send((h - 4 * i) * 8 + 7)
+
+    build_rows(
+        splat_ref, position_ref, harmonics_ref, cams_ref, surfels, basis, dirs, mask, tmp,
+        lambda h, i: request_own(h, i) if i == 3 else request(h, i),
+    )
+    between = nothing
+    for i in range(4):
+        plane = wait_plane(got, me, i, -1, send_sem.at[0], ask_sem)
+        fetch_rows(plane, got, rows, surfels, between)
+        sender = plane_sender(rows, recv, me, i, -1, send_sem.at[1], row_sem)
+        between = between_of(sender)
+    send_plane(sender)
+    recv[me] = rows[me]
+    constants(before, sign, after, mono_col)
+    for load in loads[6:8]:
+        load.wait()
+    for i in range(4):
+        arrange_rows(wait_plane(recv, me, i, 1, send_sem.at[1], row_sem), recv, table)
     composite(
         pos, counts_ref, color_ref, normal_ref, loss_ref, table, grads, before, sign, after, mono_col
     )
-    make_and_send(
-        lambda step: return_rows(step, slot, grad_rows, grads),
-        grad_rows, back, me, send_sem.at[2], recv_sem.at[2],
-    )
-    acc[...] = jnp.zeros_like(acc)
-
-    def add(step, c):
-        sum_rows(step, back, got, acc)
-        return c
-
-    lax.fori_loop(0, 8, add, 0)
-    finish_grads(position_ref, harmonics_ref, cams_ref, gs_ref, gp_ref, gh_ref, acc)
+    between = nothing
+    for i in range(4):
+        sender = plane_sender(grad_rows, back, me, i, 1, send_sem.at[2], back_sem)
+        return_rows(sender[2], slot, grad_rows, grads, between)
+        between = between_of(sender)
+    back[me] = grad_rows[me]
+    for i in range(4):
+        plane = wait_plane(back, me, i, -1, send_sem.at[2], back_sem)
+        sum_rows(plane, back, got, acc, between if i == 0 else nothing)
+    for n, ref in enumerate((ask, rows, grad_rows)):
+        blocks_of(ref, N_DEV - 1, me, send_sem.at[n], ask_sem.at[0]).wait_send()
+
+
+def finish_kernel(
+    harmonics_ref, basis, dirs, mask, acc, loss_ref, gs_ref, gp_ref, gh_ref, total_ref, tmp
+):
+    parts = stack([p.astype(F32) for p in split3(loss_ref[...])]).astype(BF16)
+    sums = dot_nt(jnp.full((16, 128), 1.0, BF16), parts)
+    total_ref[...] = sums[0:1, 0:32] + sums[0:1, 32:64] + sums[0:1, 64:96]
+    finish_grads(harmonics_ref, basis, dirs, mask, tmp, gs_ref, gp_ref, gh_ref, acc)
 
 
 VM = pl.BlockSpec(memory_space=pltpu.VMEM)
-SM = pl.BlockSpec(memory_space=pltpu.SMEM)
-LIMIT = 48 * 1024 * 1024
+LIMIT = 62 * 1024 * 1024
 
 
 def on_device(
     splat, position, harmonics, cameras, tile_lists, tile_counts, target_color, target_normal
 ):
-    gs, gp, gh, loss = pl.pallas_call(
+    acc, basis, dirs, mask, loss = pl.pallas_call(
         step_kernel,
         out_shape=(
-            jax.ShapeDtypeStruct((11, SURF), F32),
-            jax.ShapeDtypeStruct((3, SURF), F32),
-            jax.ShapeDtypeStruct((48, SURF), F32),
+            jax.ShapeDtypeStruct((4, 256, 256), F32),
+            jax.ShapeDtypeStruct((4, 16, SURF), F32),
+            jax.ShapeDtypeStruct((4, 4, SURF), F32),
+            jax.ShapeDtypeStruct((12, SURF), F32),
             jax.ShapeDtypeStruct((TILES, 128), F32),
         ),
-        in_specs=[VM, VM, VM, VM, VM, SM, VM, VM],
-        out_specs=(VM, VM, VM, VM),
+        in_specs=[pl.BlockSpec(memory_space=pltpu.HBM)] * 8,
+        out_specs=(VM,) * 5,
         scratch_shapes=[
+            pltpu.VMEM((11, SURF), F32),
+            pltpu.VMEM((3, SURF), F32),
+            pltpu.VMEM((48, SURF), F32),
+            pltpu.VMEM((4, 3), F32),
+            pltpu.VMEM((TILES, 256), I32),
+            pltpu.SMEM((TILES,), I32),
+            pltpu.VMEM((3, TILES, 256), F32),
+            pltpu.VMEM((3, TILES, 256), F32),
             pltpu.VMEM((N_DEV, 1, 128), I32),
             pltpu.VMEM((N_DEV, 1, 128), I32),
             pltpu.VMEM((N_DEV, 1, 128), I32),
@@ -627,24 +743,41 @@
             pltpu.VMEM((N_DEV, 8, 128), F32),
             pltpu.VMEM((N_DEV, 8, 128), F32),
             pltpu.VMEM((N_DEV, 8, 128), F32),
-            pltpu.VMEM((256, 256), BF16),
-            pltpu.VMEM((4, 256, 768), BF16),
+            pltpu.VMEM((256, 384), BF16),
+            pltpu.VMEM((4, 256, 512), BF16),
             pltpu.VMEM((384, 512), BF16),
             pltpu.VMEM((512, 512), BF16),
-            pltpu.VMEM((4, 256, 256), F32),
             pltpu.VMEM((512, 256), BF16),
             pltpu.VMEM((512, 256), BF16),
             pltpu.VMEM((512, 256), BF16),
             pltpu.VMEM((256, 128), BF16),
+            pltpu.VMEM((256, 128), F32),
+            pltpu.SemaphoreType.DMA((8,)),
             pltpu.SemaphoreType.DMA((3,)),
-            pltpu.SemaphoreType.DMA((3,)),
+            pltpu.SemaphoreType.DMA((8,)),
+            pltpu.SemaphoreType.DMA((8,)),
+            pltpu.SemaphoreType.DMA((8,)),
         ],
         compiler_params=pltpu.CompilerParams(
             collective_id=0, has_side_effects=True, vmem_limit_bytes=LIMIT
         ),
         name="surfel_step",
     )(splat, position, harmonics, cameras, tile_lists, tile_counts, target_color, target_normal)
-    return gs, gp, gh, jnp.sum(loss, axis=1)
+    gs, gp, gh, total = pl.pallas_call(
+        finish_kernel,
+        out_shape=(
+            jax.ShapeDtypeStruct((11, SURF), F32),
+            jax.ShapeDtypeStruct((3, SURF), F32),
+            jax.ShapeDtypeStruct((48, SURF), F32),
+            jax.ShapeDtypeStruct((1, TILES), F32),
+        ),
+        in_specs=[VM] * 6,
+        out_specs=(VM,) * 4,
+        scratch_shapes=[pltpu.VMEM((256, 128), F32)],
+        compiler_params=pltpu.CompilerParams(vmem_limit_bytes=LIMIT),
+        name="surfel_finish",
+    )(harmonics, basis, dirs, mask, acc, loss)
+    return gs, gp, gh, total.reshape(TILES)
 
 
 def solution(mesh):

time: 90.6 us -> 73.8 us (0.81)
  local copies, waits for them, and re-layouts: 9 us -> 0 us
  Pallas kernels: 79.9 us -> 73 us
    unnamed x19 -> x0, local copies, waits for them, and re-layouts: 9 us -> none
    pallas_call x1 -> x2, Pallas kernels: 79.9 us -> 73 us  [the longest x1 68.5 us: on_device(): pl.pallas_call(step_kernel, out_shape=(jax.ShapeDtypeStruct((4, 256, 256)...]
where the time goes in v3:
time: 73.8 us; the launch traced here: 73.7 us
  Pallas kernels  73 us (99%)
    pallas_call x1, Pallas kernels, on_device(): pl.pallas_call(step_kernel, out_shape=(jax.ShapeDtypeStruct((4, 256, 256)...  68.5 us
    pallas_call x1, Pallas kernels, on_device(): pl.pallas_call(finish_kernel, out_shape=(jax.ShapeDtypeStruct((11, SURF),...  4.52 us

profile of v3, /device:TPU:1, one launch (start us, length us, event | category | flops | bytes accessed | tf_op | source)
XLA Modules:
  0.0 73.7 jit_solution(13458902669186305573)
XLA Ops:
  0.6 68.5 %surfel_step.1 = (f32[4,256,256]{2,1,0:T(8,128)}, f32[4,16,4096]{2,1,0:T(8,128)}, f32[4,4,4096]{2,1,0:T(4,128)}, f32[12,4096]{1,0:T(8,128)}, f32[32,128]{1,0:T(8,128)}) custom-call(f32[11,4096]{1,0:T(8,128)} %splat_hbm.1, f32[3,4096]{1,0:T(4,128)} %position_hbm.1, f32[48,4096]{1,0:T(8,128)} %harmonics_ref.1, f32[4,3]{1,0:T(4,128)} %cams_hbm.1, ...), custom_call_target="tpu_custom_call" | custom-call | tf_op jit(solution)/shard_map/surfel_step/pallas_call | solution.py:718
  69.1 4.5 %surfel_finish.1 = (f32[11,4096]{1,0:T(8,128)}, f32[3,4096]{1,0:T(4,128)}, f32[48,4096]{1,0:T(8,128)}, f32[1,32]{1,0:T(1,128)}) custom-call(f32[48,4096]{1,0:T(8,128)} %harmonics_ref.1, f32[4,16,4096]{2,1,0:T(8,128)} %get-tuple-element.13.basis, f32[4,4,4096]{2,1,0:T(4,128)} %get-tuple-element.14.dirs, f32[12,4096]{1,0:T(8,128)} %get-tuple-element.15.mask, ...), custom_call_target="tpu_custom_call" | custom-call | tf_op jit(solution)/shard_map/surfel_finish/pallas_call | solution.py:766

commit v4 on v3

--- a/solution.py
+++ b/solution.py
@@ -165,7 +165,7 @@
 def message_blocks(ref, first):
     pieces = []
     for s in range(8):
-        tile = ref[first + s]
+        tile = jnp.concatenate([ref[first + s], jnp.zeros((1, 128), F32)], axis=0)
         pieces.append(
             jnp.concatenate([shift(tile, SHARE * s), shift(tile, SHARE * s + 64)], axis=0)
         )
@@ -176,7 +176,7 @@
     for s, piece in enumerate(split_eight(blocks)):
         ref[first + s] = jnp.where(
             lane_of(piece[0:8]) < 64, piece[0:8], pltpu.roll(piece[8:16], 64, 1)
-        )
+        )[0:7]
 
 
 def wide(blocks):
@@ -213,11 +213,12 @@
     holder_id = iota((N_DEV, 256), 0)
     lane = iota((1, 256), 1)
     rank_id = iota((N_DEV, 256), 0) & 63
-    group = 4
-
-    def tiles(i, state):
+    group = 8
+
+    def tiles(i, state, greets):
         carry, sums = state
-        greet(i)
+        if greets:
+            greet(i)
         flats = [lists_ref[pl.ds(i * group + u, 1), :] for u in range(group)]
         lives = [lane < counts_ref[i * group + u] for u in range(group)]
         holders = [jnp.where(lives[u], flats[u] // SURF, -1) for u in range(group)]
@@ -245,9 +246,9 @@
         sums = sums + dot_nt(jnp.concatenate(left, axis=1), jnp.concatenate(right, axis=1))
         return carry, sums
 
-    _, sums = lax.fori_loop(
-        0, TILES // group, tiles, (jnp.zeros((N_DEV, 128), F32), jnp.zeros((3 * N_DEV, 128), F32))
-    )
+    state = (jnp.zeros((N_DEV, 128), F32), jnp.zeros((3 * N_DEV, 128), F32))
+    state = lax.fori_loop(0, 2, lambda i, c: tiles(i, c, True), state)
+    _, sums = lax.fori_loop(2, TILES // group, lambda i, c: tiles(i, c, False), state)
     named = (iota((N_DEV, 128), 1) & 63) < SHARE
     low = sums[128:256].astype(I32)
     local = (sums[0:128].astype(I32) + 256) * 8 + low // TILES
@@ -298,11 +299,12 @@
                     value > 0.0, 1.0, jnp.where(value == 0.0, 0.5, 0.0)
                 )
                 colors.append(jnp.maximum(value, 0.0))
-            rows = jnp.concatenate([splat] + colors + [jnp.zeros((2, 256), F32)], axis=0)
+            zero = jnp.zeros((1, 256), F32)
+            rows = jnp.concatenate([splat[0:7], zero, splat[7:11]] + colors + [zero], axis=0)
             table[v, pl.ds(pl.multiple_of(h * 16, 16), 16), :] = jnp.concatenate(split2(rows), axis=1)
 
     for i in range(4):
-        lax.fori_loop(4 * i, 4 * i + 4, lambda h, c: build(h, i) or c, 0)
+        lax.fori_loop(4 * i, 4 * i + 4, lambda h, c: build(h, i) or c, 0, unroll=True)
 
 
 def plane_blocks(blocks_of_eight, ref, plane):
@@ -350,13 +352,18 @@
         table[pl.ds(pl.multiple_of(plane * 96 + n * 16, 16), 16), :] = beside(split2(g))
 
 
-def constants(before, sign, after, mono_col):
-    j, k = iota((512, 256), 0) & 255, iota((512, 256), 1)
-    before[...] = jnp.where(j < k, 1.0, 0.0).astype(BF16)
-    sign[...] = jnp.where(j < k, 1.0, jnp.where(j > k, -1.0, 0.0)).astype(BF16)
-    after[...] = jnp.where(j > k, 1.0, 0.0).astype(BF16)
+def constants(before, sign, after, mono_col, between):
+    for n in range(4):
+        rows = slice(n * 128, n * 128 + 128)
+        j, k = (iota((128, 256), 0) + n * 128) & 255, iota((128, 256), 1)
+        before[rows, :] = jnp.where(j < k, 1.0, 0.0).astype(BF16)
+        sign[rows, :] = jnp.where(j < k, 1.0, jnp.where(j > k, -1.0, 0.0)).astype(BF16)
+        after[rows, :] = jnp.where(j > k, 1.0, 0.0).astype(BF16)
+        between(n)
     col = iota((256, 128), 1)
+    between(4)
     mono_col[...] = jnp.where(col < 24, monomials(iota((256, 128), 0), col & 7), 0.0).astype(BF16)
+    between(5)
 
 
 def composite(
@@ -364,10 +371,12 @@
 ):
     lane = iota((1, 256), 1)
     row8 = iota((8, 256), 0)
-    y_scale = jnp.where(row8 < 3, -0.25, jnp.where(row8 < 6, 1.0, 0.0))
-    y_const = jnp.where(row8 == 6, 0.25, 0.0)
+    normal_row = (row8 > 0) & (row8 < 4)
+    color_row = (row8 > 3) & (row8 < 7)
+    y_scale = jnp.where(normal_row, -0.25, jnp.where(color_row, 1.0, 0.0))
+    y_const = jnp.where(row8 == 0, 0.25, 0.0)
     kappa = 2.0 / 256.0
-    dv_scale = jnp.where(row8 < 3, -0.25 * kappa, jnp.where(row8 < 6, kappa, 0.0))
+    dv_scale = jnp.where(normal_row, -0.25 * kappa, jnp.where(color_row, kappa, 0.0))
     px_low = (row8.astype(F32) - 7.5) * 0.125
     px_high = px_low + 1.0
     zero1 = jnp.zeros((1, 256), F32)
@@ -400,7 +409,7 @@
                 ]
             )
             coefs.append(stack([p.astype(F32) for p in split3(coef)] + [zero8]).astype(BF16))
-        depth = [rows[u][7:8] for u in each]
+        depth = [rows[u][8:9] for u in each]
         v8 = [rows[u][8:16] for u in each]
         alpha = [jnp.exp2(dot_nn(mono_col[:, 0:32], coefs[u])) for u in each]
         logkeep = [jnp.log(1.0 - alpha[u]) for u in each]
@@ -420,9 +429,9 @@
             v16 = stack([p.astype(F32) for p in split2(v8[u])]).astype(BF16)
             shown = dot_nt(beside([v16, v16]), w2[u])
             shown = shown[0:8] + shown[8:16]
-            resid.append(shown[3:6] - color_ref[:, t, :])
+            resid.append(shown[4:7] - color_ref[:, t, :])
         for u, t in enumerate(ts):
-            x8 = stack([normal_ref[:, t, :], resid[u], zero1 + 1.0, zero1])
+            x8 = stack([zero1 + 1.0, normal_ref[:, t, :], resid[u], zero1])
             xh, xl = [p.astype(F32) for p in split2(x8)]
             yh, yl = [p.astype(F32) for p in split2(v8[u] * y_scale + y_const)]
             x32.append(stack([xh, xl, xh, zero8]).astype(BF16))
@@ -471,16 +480,16 @@
                     b0 * m1 + b1 * m3 + b2 * m4,
                     b0 * m2 + b1 * m4 + b2 * m5,
                     (sigs[u] - 1.0) * m0,
-                    kappa * ga,
-                    dv * dv_scale,
+                    zero1,
+                    dv * dv_scale + jnp.where(row8 == 0, kappa * ga, 0.0),
                 ]
             )
             grads[pl.ds(pl.multiple_of(t * 16, 16), 16), :] = beside(split2(out))
-            facing = v8[u][0:3] * dv[0:3]
+            facing = v8[u][1:4] * dv[1:4]
             loss = (
                 jnp.sum(resid[u] * resid[u] - 0.5 * facing, axis=0, keepdims=True)
                 + 2.0 * (depth[u] * ga)
-                + 0.5 * dv[6:7]
+                + 0.5 * dv[0:1]
             ) * (1.0 / 256.0)
             loss_ref[pl.ds(t, 1), :] = loss[:, 0:128] + loss[:, 128:256]
         return c
@@ -512,9 +521,10 @@
         lanes = pl.ds(pl.multiple_of(h * 256, 256), 256)
         views = [acc[v, pl.ds(pl.multiple_of(h * 16, 16), 16), :] for v in range(4)]
         total = (views[0] + views[1]) + (views[2] + views[3])
-        gs_ref[:, lanes] = total[0:11]
+        gs_ref[0:7, lanes] = total[0:7]
+        gs_ref[7:11, lanes] = total[8:12]
         dcol = [
-            [views[v][11 + ch : 12 + ch] * mask_ref[ch * 4 + v : ch * 4 + v + 1, lanes] for v in range(4)]
+            [views[v][12 + ch : 13 + ch] * mask_ref[ch * 4 + v : ch * 4 + v + 1, lanes] for v in range(4)]
             for ch in range(3)
         ]
         basis = [basis_ref[v, :, lanes] for v in range(4)]
@@ -538,20 +548,11 @@
     lax.fori_loop(0, 16, finish, 0)
 
 
-def greet_all(me):
+def greet_some(me, first, count):
     barrier = pltpu.get_barrier_semaphore()
-
-    def greet(i, c):
-        for s in range(1, 16):
-            pl.semaphore_signal(
-                barrier, inc=1, device_id=(lax.rem(me + i * 15 + s, N_DEV),), device_id_type=MESH
-            )
-        return c
-
-    lax.fori_loop(0, 8, greet, 0)
-    for s in range(121, N_DEV):
+    for n in range(count):
         pl.semaphore_signal(
-            barrier, inc=1, device_id=(lax.rem(me + s, N_DEV),), device_id_type=MESH
+            barrier, inc=1, device_id=(lax.rem(me + first + n, N_DEV),), device_id_type=MESH
         )
 
 
@@ -603,16 +604,6 @@
     return between
 
 
-def send_plane(sender):
-    send, count, _ = sender
-
-    def one(s, c):
-        send(s)
-        return c
-
-    lax.fori_loop(0, count, one, 0)
-
-
 def nothing(n):
     pass
 
@@ -625,10 +616,11 @@
 
 def step_kernel(
     splat_hbm, position_hbm, harmonics_hbm, cams_hbm, lists_hbm, counts_hbm, color_hbm, normal_hbm,
-    acc, basis, dirs, mask, loss_ref,
+    acc_hbm, basis_hbm, dirs_hbm, mask_hbm, loss_ref,
     splat_ref, position_ref, harmonics_ref, cams_ref, lists_ref, counts_ref, color_ref, normal_ref,
     ask, got, slot, pos, rows, recv, grad_rows, back, upper, surfels, table, grads,
-    before, sign, after, mono_col, tmp, load_sem, send_sem, ask_sem, row_sem, back_sem,
+    before, sign, after, mono_col, tmp, acc, basis, dirs, mask,
+    load_sem, send_sem, ask_sem, row_sem, back_sem, store_sem,
 ):
     me = lax.axis_index("surf")
     pairs = [
@@ -641,10 +633,12 @@
     ]
     for load in loads:
         load.start()
-    greet_all(me)
+    greet_some(me, 127, 1)
     loads[0].wait()
     loads[1].wait()
-    route(lists_ref, counts_ref, ask, slot, pos, upper, nothing)
+    route(
+        lists_ref, counts_ref, ask, slot, pos, upper, lambda i: greet_some(me, i * 63 + 1, 63)
+    )
     pl.semaphore_wait(pltpu.get_barrier_semaphore(), N_DEV - 1)
     got[me] = ask[me]
     for load in loads[2:6]:
@@ -670,15 +664,20 @@
         splat_ref, position_ref, harmonics_ref, cams_ref, surfels, basis, dirs, mask, tmp,
         lambda h, i: request_own(h, i) if i == 3 else request(h, i),
     )
+    stores = [
+        pltpu.make_async_copy(src, dst, store_sem.at[n])
+        for n, (src, dst) in enumerate(((basis, basis_hbm), (dirs, dirs_hbm), (mask, mask_hbm)))
+    ]
+    for store in stores:
+        store.start()
     between = nothing
     for i in range(4):
         plane = wait_plane(got, me, i, -1, send_sem.at[0], ask_sem)
         fetch_rows(plane, got, rows, surfels, between)
         sender = plane_sender(rows, recv, me, i, -1, send_sem.at[1], row_sem)
         between = between_of(sender)
-    send_plane(sender)
     recv[me] = rows[me]
-    constants(before, sign, after, mono_col)
+    constants(before, sign, after, mono_col, between)
     for load in loads[6:8]:
         load.wait()
     for i in range(4):
@@ -695,8 +694,12 @@
     for i in range(4):
         plane = wait_plane(back, me, i, -1, send_sem.at[2], back_sem)
         sum_rows(plane, back, got, acc, between if i == 0 else nothing)
+        stores.append(pltpu.make_async_copy(acc.at[plane], acc_hbm.at[plane], store_sem.at[3 + i]))
+        stores[-1].start()
     for n, ref in enumerate((ask, rows, grad_rows)):
         blocks_of(ref, N_DEV - 1, me, send_sem.at[n], ask_sem.at[0]).wait_send()
+    for store in stores:
+        store.wait()
 
 
 def finish_kernel(
@@ -725,7 +728,7 @@
             jax.ShapeDtypeStruct((TILES, 128), F32),
         ),
         in_specs=[pl.BlockSpec(memory_space=pltpu.HBM)] * 8,
-        out_specs=(VM,) * 5,
+        out_specs=(pl.BlockSpec(memory_space=pltpu.HBM),) * 4 + (VM,),
         scratch_shapes=[
             pltpu.VMEM((11, SURF), F32),
             pltpu.VMEM((3, SURF), F32),
@@ -739,10 +742,10 @@
             pltpu.VMEM((N_DEV, 1, 128), I32),
             pltpu.VMEM((N_DEV, 1, 128), I32),
             pltpu.VMEM((TILES, 256), I32),
-            pltpu.VMEM((N_DEV, 8, 128), F32),
-            pltpu.VMEM((N_DEV, 8, 128), F32),
-            pltpu.VMEM((N_DEV, 8, 128), F32),
-            pltpu.VMEM((N_DEV, 8, 128), F32),
+            pltpu.VMEM((N_DEV, 7, 128), F32),
+            pltpu.VMEM((N_DEV, 7, 128), F32),
+            pltpu.VMEM((N_DEV, 7, 128), F32),
+            pltpu.VMEM((N_DEV, 7, 128), F32),
             pltpu.VMEM((256, 384), BF16),
             pltpu.VMEM((4, 256, 512), BF16),
             pltpu.VMEM((384, 512), BF16),
@@ -752,11 +755,16 @@
             pltpu.VMEM((512, 256), BF16),
             pltpu.VMEM((256, 128), BF16),
             pltpu.VMEM((256, 128), F32),
+            pltpu.VMEM((4, 256, 256), F32),
+            pltpu.VMEM((4, 16, SURF), F32),
+            pltpu.VMEM((4, 4, SURF), F32),
+            pltpu.VMEM((12, SURF), F32),
             pltpu.SemaphoreType.DMA((8,)),
             pltpu.SemaphoreType.DMA((3,)),
             pltpu.SemaphoreType.DMA((8,)),
             pltpu.SemaphoreType.DMA((8,)),
             pltpu.SemaphoreType.DMA((8,)),
+            pltpu.SemaphoreType.DMA((7,)),
         ],
         compiler_params=pltpu.CompilerParams(
             collective_id=0, has_side_effects=True, vmem_limit_bytes=LIMIT

time: 73.8 us -> 72.8 us (0.986)
  Pallas kernels: 73 us -> 72.1 us
    pallas_call x1, Pallas kernels: 68.5 us -> 67.5 us  [on_device(): pl.pallas_call(step_kernel, out_shape=(jax.ShapeDtypeStruct((4, 256, 256)...]
where the time goes in v4:
time: 72.8 us; the launch traced here: 72.7 us
  Pallas kernels  72.1 us (99%)
    pallas_call x1, Pallas kernels, on_device(): pl.pallas_call(step_kernel, out_shape=(jax.ShapeDtypeStruct((4, 256, 256)...  67.5 us
    pallas_call x1, Pallas kernels, on_device(): pl.pallas_call(finish_kernel, out_shape=(jax.ShapeDtypeStruct((11, SURF),...  4.53 us

profile of v4, /device:TPU:1, one launch (start us, length us, event | category | flops | bytes accessed | tf_op | source)
XLA Modules:
  0.0 72.7 jit_solution(7278402302032452063)
XLA Ops:
  0.6 67.5 %surfel_step.1 = (f32[4,256,256]{2,1,0:T(8,128)}, f32[4,16,4096]{2,1,0:T(8,128)}, f32[4,4,4096]{2,1,0:T(4,128)}, f32[12,4096]{1,0:T(8,128)}, f32[32,128]{1,0:T(8,128)}) custom-call(f32[11,4096]{1,0:T(8,128)} %splat_hbm.1, f32[3,4096]{1,0:T(4,128)} %position_hbm.1, f32[48,4096]{1,0:T(8,128)} %harmonics_ref.1, f32[4,3]{1,0:T(4,128)} %cams_hbm.1, ...), custom_call_target="tpu_custom_call" | custom-call | tf_op jit(solution)/shard_map/surfel_step/pallas_call | solution.py:721
  68.2 4.5 %surfel_finish.1 = (f32[11,4096]{1,0:T(8,128)}, f32[3,4096]{1,0:T(4,128)}, f32[48,4096]{1,0:T(8,128)}, f32[1,32]{1,0:T(1,128)}) custom-call(f32[48,4096]{1,0:T(8,128)} %harmonics_ref.1, f32[4,16,4096]{2,1,0:T(8,128)} %get-tuple-element.13.basis, f32[4,4,4096]{2,1,0:T(4,128)} %get-tuple-element.14.dirs, f32[12,4096]{1,0:T(8,128)} %get-tuple-element.15.mask, ...), custom_call_target="tpu_custom_call" | custom-call | tf_op jit(solution)/shard_map/surfel_finish/pallas_call | solution.py:774
